TPU v7x, 128 devices: a whole 4x4x4 slice. The times are simulated.
128 devices in a mesh: sec: 8 (over z_lo, x), tile: 16 (over z_hi, y, core).
Axes of the slice: x: 4, y: 4, z: 4 (z_hi: 2, z_lo: 2; z = z_hi * 2 + z_lo), core: 2. Of those that a mesh axis runs over, the one named last changes fastest.
Arguments:
- sections: bfloat16 [8, 2048, 2048], P('sec', None, 'tile'), may hold values from -6 to 6
- tile_shift: int32 [8, 16, 4, 2], P('sec', 'tile'), may hold values from -4 to 4
- w_first: bfloat16 [2, 2, 1, 32], replicated, may hold values from -4 to 4
- w_second: bfloat16 [2, 2, 32, 64], replicated, may hold values from -0.75 to 0.75
- w_third: bfloat16 [2, 2, 64, 64], replicated, may hold values from -0.5 to 0.5
- w_fourth: bfloat16 [64, 64], replicated, may hold values from -1 to 1
- w_fifth: bfloat16 [64, 32], replicated, may hold values from -0.75 to 0.75
Outputs:
- correlation: bfloat16 [8, 256, 289, 256], P('sec', 'tile')
All inputs are finite; a program needn't handle non-finite values.
Results may differ from a plain program's by a relative error of at most 0.0058.
Values may be sent and summed in bfloat16 or wider, within the bound.
A program may use at most 192 MiB of HBM per device.

v0:
```python
import math

import jax
import jax.numpy as jnp
from jax import lax
from jax.sharding import PartitionSpec as P

CF = 32
REACH = 8
BOUND = 4
TILE = 16
TILE_W = 64
HALO = 12


def shifted(block, axis, distance):
    devices = range(lax.axis_size(axis))
    route = [(i - distance, i) for i in devices if i - distance in devices]
    return lax.ppermute(block, axis, route)


def with_halo(cells, sides, width):
    for axis, dim in sides:
        count = lax.axis_size(axis)
        ends = count - 1
        head = lax.slice_in_dim(cells, 0, width, axis=dim)
        tail = lax.slice_in_dim(cells, cells.shape[dim] - width, cells.shape[dim], axis=dim)
        cells = jnp.concatenate(
            [
                lax.ppermute(tail, axis, [(i, (i + 1) % count) for i in range(ends)]),
                cells,
                lax.ppermute(head, axis, [((i + 1) % count, i) for i in range(ends)]),
            ],
            axis=dim,
        )
    return cells


def first_layer(image, weight):
    rows, cols = image.shape
    paired = image.reshape(rows // 2, 2, cols // 2, 2)
    total = None
    for row_phase in range(2):
        term = jnp.einsum(
            "rck,ko->rco",
            paired[:, row_phase],
            weight[row_phase, :, 0, :],
            preferred_element_type=jnp.float32,
        )
        total = term if total is None else total + term
    return jnp.maximum(total, 0.0).astype(jnp.bfloat16)


def patch_layer(field, weight):
    rows, cols, chans = field.shape
    outs = weight.shape[3]
    paired = field.reshape(rows // 2, 2, cols // 2, 2 * chans)
    total = None
    for row_phase in range(2):
        folded = weight[row_phase].reshape(2 * chans, outs)
        term = jnp.einsum(
            "rck,ko->rco", paired[:, row_phase], folded, preferred_element_type=jnp.float32
        )
        total = term if total is None else total + term
    return jnp.maximum(total, 0.0).astype(jnp.bfloat16)


def point_layer(field, weight, relu):
    mixed = jnp.einsum("rci,io->rco", field, weight, preferred_element_type=jnp.float32)
    if relu:
        mixed = jnp.maximum(mixed, 0.0)
    return mixed.astype(jnp.bfloat16)


def encode_stack(pixels, weights):

    def encode_one(image):
        field = first_layer(image, weights[0])
        field = patch_layer(field, weights[1])
        field = patch_layer(field, weights[2])
        field = point_layer(field, weights[3], True)
        return point_layer(field, weights[4], False)

    return lax.map(encode_one, pixels)


def correlate(current, source, shifts):
    rows, cols, chans = current.shape
    span = 2 * REACH + 1
    halo = REACH + BOUND
    width = TILE_W + 2 * REACH
    padded = jnp.pad(source, ((0, 0), (halo, halo), (0, 0)))
    zero = jnp.zeros((), jnp.int32)

    def one_tile(row_tile, col_tile):
        shift_y = shifts[row_tile, col_tile, 0]
        shift_x = shifts[row_tile, col_tile, 1]
        here = lax.dynamic_slice(
            current, (row_tile * TILE, col_tile * TILE_W, zero), (TILE, TILE_W, chans)
        )
        start_y = row_tile * TILE + halo - REACH + shift_y
        start_x = col_tile * TILE_W + halo - REACH + shift_x
        window = lax.dynamic_slice(
            padded, (start_y, start_x, zero), (TILE + 2 * REACH, width, chans)
        )
        lifted = jnp.stack([window[lift : lift + TILE] for lift in range(span)], axis=1)
        products = jnp.einsum("yxc,ylwc->ylxw", here, lifted, preferred_element_type=jnp.float32)
        flat = products.reshape(TILE, span, TILE_W * width)
        flat = jnp.pad(flat, ((0, 0), (0, 0), (0, TILE_W)))
        diagonal = flat.reshape(TILE, span, TILE_W, width + 1)[..., :span]
        diagonal = jnp.transpose(diagonal, (0, 1, 3, 2))
        return diagonal.reshape(TILE, span * span, TILE_W)

    row_ids = jnp.arange(shifts.shape[0], dtype=jnp.int32)
    col_ids = jnp.arange(shifts.shape[1], dtype=jnp.int32)
    result = jax.vmap(lambda r: jax.vmap(lambda c: one_tile(r, c))(col_ids))(row_ids)
    result = (result * (1.0 / math.sqrt(CF))).astype(jnp.bfloat16)
    count_y, count_x = (shifts.shape[0], shifts.shape[1])
    result = jnp.transpose(result, (0, 2, 3, 1, 4))
    return result.reshape(count_y * TILE, span * span, count_x * TILE_W)


def local(sections, tile_shift, w_first, w_second, w_third, w_fourth, w_fifth):
    weights = (w_first, w_second, w_third, w_fourth, w_fifth)
    banded = lax.all_to_all(sections, "tile", split_axis=1, concat_axis=2, tiled=True)
    features = encode_stack(banded, weights)
    previous_last = shifted(features[-1], "sec", 1)
    stacked = jnp.concatenate([previous_last[None], features[:-1]], axis=0)
    source = with_halo(stacked, (("tile", 1),), HALO)
    return lax.map(
        lambda packed: correlate(packed[0], packed[1], packed[2]), (features, source, tile_shift)
    )


def solution(mesh):
    placed = (P("sec", None, "tile"), P("sec", "tile", None, None), P(), P(), P(), P(), P())
    return jax.shard_map(
        local, mesh=mesh, in_specs=placed, out_specs=P("sec", "tile", None, None), check_vma=False
    )
```

profile of v0, /device:TPU:33, one launch (start us, length us, event | category | flops | bytes accessed | tf_op | source)
XLA Modules:
  0.0 419.1 jit_solution(17560742242046906077)
XLA Ops:
  0.0 1.8 copy.224
  2.3 11.5 %reduce.6 = bf16[2048,128]{1,0:T(8,128)(2,1)S(1)} reduce(bf16[2048,1,128]{2,1,0:T(2,128)(2,1)S(1)} %bitcast.246, bf16[]{:T(256)} %broadcast.280), dimensions={1}, to_apply=%bitcast.215.reduce_sub_computation | reduce | bytes 1048578
  13.9 0.9 reshape.216
  14.8 7.6 %all-to-all-start = ((bf16[16,2,8192]{2,1,0:T(2,128)(2,1)}), bf16[16,2,8192]{2,1,0:T(2,128)(2,1)S(1)}, u32[]{:S(2)}, u32[]{:S(2)}) async-start(bf16[16,2,8192]{2,1,0:T(2,128)(2,1)} %reshape.216), calls=%async_computation | async-start | bytes 1048576 | tf_op jit(solution)/shard_map/all_to_all | solution.py:125
  22.8 1.3 gather_fusion
  24.2 0.7 fusion.41
  24.9 0.8 fusion.40
  25.7 8.0 %all-to-all-done = bf16[16,2,8192]{2,1,0:T(2,128)(2,1)S(1)} async-done(((bf16[16,2,8192]{2,1,0:T(2,128)(2,1)}), bf16[16,2,8192]{2,1,0:T(2,128)(2,1)S(1)}, u32[]{:S(2)}, u32[]{:S(2)}) %all-to-all-start) | async-done | bytes 524320 | tf_op jit(solution)/shard_map/all_to_all | solution.py:125
  33.7 0.5 reshape.217
  34.7 73.3 %reshape.140 = bf16[64,2,1024,2]{3,2,1,0:T(8,128)(2,1)} reshape(bf16[1,128,16,128]{3,2,1,0:T(8,128)(2,1)S(1)} %copy.156) | data formatting | bytes 1048576 | tf_op jit(solution)/shard_map/while/body/eval_jaxpr/reshape | solution.py:41
  108.0 14.5 %fusion.2 = f32[64,1024,32]{1,2,0:T(8,128)} fusion(bf16[64,2,1024,2]{3,2,1,0:T(8,128)(2,1)} %reshape.140, bf16[2,2,1,32]{3,1,2,0:T(2,128)(2,1)S(1)} %copy-done.7), kind=kOutput, calls=%fused_computation.10 | convolution fusion | flops 8388608 | bytes 25166336 | tf_op jit(solution)/shard_map/while/body/eval_jaxpr/rck,ko->rco/dot_general | solution.py:44
  122.5 12.5 %maximum_convert_fusion = bf16[64,1024,32]{1,2,0:T(8,128)(2,1)} fusion(f32[64,1024,32]{1,2,0:T(8,128)} %fusion.2, bf16[64,2,1024,2]{3,2,1,0:T(8,128)(2,1)} %reshape.140, bf16[2,2,1,32]{3,1,2,0:T(2,128)(2,1)S(1)} %copy-done.7), kind=kOutput, calls=%fused_computation.15 | convolution fusion | flops 14680064 | bytes 29360640 | tf_op jit(solution)/shard_map/while/body/eval_jaxpr/rck,ko->rco/dot_general | solution.py:44
  135.0 14.4 %copy.159 = bf16[64,1024,32]{2,1,0:T(8,128)(2,1)} copy(bf16[64,1024,32]{1,2,0:T(8,128)(2,1)} %maximum_convert_fusion) | data formatting | bytes 8388608 | tf_op jit(solution)/shard_map/while/body/eval_jaxpr/convert_element_type | solution.py:51
  149.4 21.5 %reshape.141 = bf16[32,2,512,64]{3,2,1,0:T(8,128)(2,1)} reshape(bf16[64,1024,32]{2,1,0:T(8,128)(2,1)} %copy.159) | data formatting | bytes 8388608 | tf_op jit(solution)/shard_map/while/body/eval_jaxpr/reshape | solution.py:57
  170.9 4.0 fusion.5
  174.8 0.7 copy-done.3
  175.5 1.6 maximum_convert_fusion.1
  177.2 3.2 copy.164
  180.4 5.0 %reshape.142 = bf16[16,2,256,128]{3,2,1,0:T(8,128)(2,1)S(1)} reshape(bf16[32,512,64]{2,1,0:T(8,128)(2,1)} %copy.164) | data formatting | bytes 4194304 | tf_op jit(solution)/shard_map/while/body/eval_jaxpr/reshape | solution.py:57
  186.0 1.5 fusion.9
  187.5 1.3 convolution_convert_fusion
  188.8 3.1 collective-permute-start
  192.1 0.6 gather_fusion.1
  192.8 6.7 %collective-permute-done = bf16[16,256,32]{1,2,0:T(8,128)(2,1)S(1)} collective-permute-done((bf16[16,256,32]{1,2,0:T(8,128)(2,1)S(1)}, bf16[16,256,32]{1,2,0:T(8,128)(2,1)S(1)}, u32[]{:S(2)}, u32[]{:S(2)}) %collective-permute-start) | collective-permute-done | bytes 262176 | tf_op jit(solution)/shard_map/ppermute | solution.py:19
  199.5 3.3 collective-permute-start.1
  202.8 1.9 collective-permute-start.2
  205.2 0.9 copy.192
  206.1 1.7 gather_fusion.2
  207.8 2.1 collective-permute-done.2
  210.3 11.1 %while.1 = (s32[]{:T(128)}, bf16[40,280,32]{1,2,0:T(8,128)(2,1)S(1)}, s32[4,3]{1,0:T(4,128)S(1)}, bf16[4,32,80,32]{2,3,1,0:T(8,128)(2,1)S(1)}, s32[]{:T(128)}) while((s32[]{:T(128)}, bf16[40,280,32]{1,2,0:T(8,128)(2,1)S(1)}, s32[4,3]{1,0:T(4,128)S(1)}, bf16[4,32,80,32]{2,3,1,0:T(8,128)(2,1)S(1)}, s32[]{:T(128)}) %tuple.37), condition=%wide.while_cond, body=%wide.while_body.sunk | while | flops 2 | bytes 1507453 | solution.py:103
  210.6 0.6 fusion.48
  211.2 1.4 constant_dynamic-slice_fusion.5
  213.3 0.6 fusion.48
  213.9 1.4 constant_dynamic-slice_fusion.5
  216.0 0.6 fusion.48
  216.7 1.4 constant_dynamic-slice_fusion.5
  218.7 0.6 fusion.48
  219.4 1.4 constant_dynamic-slice_fusion.5
  222.7 3.5 copy-done.4
  226.2 17.5 %convolution_bitcast_fusion = f32[1,4,16,17,64,80]{5,4,3,2,1,0:T(8,128)} fusion(bf16[1,4,16,17,80,32]{4,5,3,2,1,0:T(8,128)(2,1)} %copy-done.4, bf16[4,16,64,32,1]{3,1,2,0,4:T(8,128)(2,1)S(1)} %bitcast.244), kind=kOutput, calls=%fused_computation.13 | convolution fusion | flops 356515840 | bytes 28114944 | tf_op jit(solution)/shard_map/while/body/eval_jaxpr/vmap(vmap(yxc,ylwc->ylxw))/dot_general | solution.py:107
  243.7 42.2 %reshape.211 = f32[1,4,16,17,5120]{4,3,2,1,0:T(8,128)} reshape(f32[1,4,16,17,64,80]{5,4,3,2,1,0:T(8,128)} %convolution_bitcast_fusion) | data formatting | bytes 44564480 | tf_op jit(solution)/shard_map/while/body/eval_jaxpr/vmap(vmap())/reshape | solution.py:108
  285.9 20.2 %copy.209 = f32[1,4,16,17,5120]{4,2,3,1,0:T(8,128)S(1)} copy(f32[1,4,16,17,5120]{4,3,2,1,0:T(8,128)} %reshape.211) | data formatting | bytes 44564480 | tf_op jit(solution)/shard_map/while/body/eval_jaxpr/vmap(vmap())/reshape | solution.py:108
  306.1 7.9 %pad.11 = f32[1,4,16,17,5184]{4,2,3,1,0:T(8,128)} pad(f32[1,4,16,17,5120]{4,2,3,1,0:T(8,128)S(1)} %copy.209, f32[]{:T(128)} %constant.32.clone.1), padding=0_0x0_0x0_0x0_0x0_64 | pad | bytes 44843012 | tf_op jit(solution)/shard_map/while/body/eval_jaxpr/vmap(vmap(jit(_pad)))/pad | solution.py:109
  314.0 59.4 %reshape.146 = f32[1,4,16,17,64,81]{5,4,2,3,1,0:T(8,128)} reshape(f32[1,4,16,17,5184]{4,2,3,1,0:T(8,128)} %pad.11) | data formatting | bytes 45121536 | tf_op jit(solution)/shard_map/while/body/eval_jaxpr/vmap(vmap())/reshape | solution.py:110
  373.5 19.5 %fusion.1 = bf16[1,4,16,17,17,64]{4,5,2,3,1,0:T(8,128)(2,1)} fusion(f32[1,4,16,17,64,81]{5,4,2,3,1,0:T(8,128)} %reshape.146), kind=kLoop, calls=%fused_computation.8 | loop fusion | flops 2367488 | bytes 7102464 | tf_op jit(solution)/shard_map/while/body/eval_jaxpr/convert_element_type | solution.py:117
  392.9 16.8 %copy.195 = bf16[1,4,16,17,17,64]{5,2,4,3,1,0:T(8,128)(2,1)} copy(bf16[1,4,16,17,17,64]{4,5,2,3,1,0:T(8,128)(2,1)} %fusion.1) | data formatting | bytes 4734976 | tf_op jit(solution)/shard_map/while/body/eval_jaxpr/convert_element_type | solution.py:117
  409.7 6.3 %copy.196 = bf16[1,16,289,4,64]{2,4,3,1,0:T(8,128)(2,1)S(1)} copy(bf16[1,16,289,4,64]{4,1,2,3,0:T(8,128)(2,1)} %bitcast.242) | data formatting | bytes 4734976 | tf_op jit(solution)/shard_map/while/body/eval_jaxpr/transpose | solution.py:119
  416.1 3.1 copy.197
  (70 shorter events, 6.8 us)
Async XLA Ops:
  0.0 186.0 %copy-start = (bf16[64,64]{1,0:T(8,128)(2,1)S(1)}, bf16[64,64]{1,0:T(8,128)(2,1)}, u32[]{:S(2)}) copy-start(bf16[64,64]{1,0:T(8,128)(2,1)} %param.12) | copy-start | bytes 24580
  14.8 19.0 %all-to-all-start = ((bf16[16,2,8192]{2,1,0:T(2,128)(2,1)}), bf16[16,2,8192]{2,1,0:T(2,128)(2,1)S(1)}, u32[]{:S(2)}, u32[]{:S(2)}) async-start(bf16[16,2,8192]{2,1,0:T(2,128)(2,1)} %reshape.216), calls=%async_computation | async-start | bytes 1048576 | tf_op jit(solution)/shard_map/all_to_all | solution.py:125
  34.7 73.3 %copy-start.7 = (bf16[2,2,1,32]{3,1,2,0:T(2,128)(2,1)S(1)}, bf16[2,2,1,32]{3,1,2,0:T(2,128)(2,1)}, u32[]{:S(2)}) copy-start(bf16[2,2,1,32]{3,1,2,0:T(2,128)(2,1)} %param.9) | copy-start | bytes 772
  170.9 4.6 %copy-start.3 = (bf16[32,2,512,64]{3,2,1,0:T(8,128)(2,1)S(1)}, bf16[32,2,512,64]{3,2,1,0:T(8,128)(2,1)}, u32[]{:S(2)}) copy-start(bf16[32,2,512,64]{3,2,1,0:T(8,128)(2,1)} %reshape.141) | copy-start | bytes 12582916
  177.2 10.3 %copy-start.6 = (bf16[64,32]{0,1:T(8,128)(2,1)S(1)}, bf16[64,32]{0,1:T(8,128)(2,1)}, u32[]{:S(2)}) copy-start(bf16[64,32]{0,1:T(8,128)(2,1)} %param.13) | copy-start | bytes 12292
  177.2 14.9 %copy-start.2 = (s32[1,1,4,2]{2,3,1,0:T(2,128)S(1)}, s32[1,1,4,2]{2,3,1,0:T(2,128)}, u32[]{:S(2)}) copy-start(s32[1,1,4,2]{2,3,1,0:T(2,128)} %param.8) | copy-start | bytes 100
  188.8 10.7 %collective-permute-start = (bf16[16,256,32]{1,2,0:T(8,128)(2,1)S(1)}, bf16[16,256,32]{1,2,0:T(8,128)(2,1)S(1)}, u32[]{:S(2)}, u32[]{:S(2)}) collective-permute-start(bf16[16,256,32]{1,2,0:T(8,128)(2,1)S(1)} %convolution_convert_fusion), channel_id=1, source_target_pairs={{0,16},{16,32},{32,48},{48,64},{64,80},{80,96},{96,112},{1,17},{17... | collective-permute-start | bytes 786440 | tf_op jit(solution)/shard_map/ppermute | solution.py:19
  199.5 8.2 %collective-permute-start.1 = (bf16[1,12,256,32]{2,3,1,0:T(8,128)(2,1)S(1)}, bf16[1,12,256,32]{2,3,1,0:T(8,128)(2,1)S(1)}, u32[]{:S(2)}, u32[]{:S(2)}) collective-permute-start(bf16[1,12,256,32]{2,3,1,0:T(8,128)(2,1)S(1)} %get-tuple-element.82), channel_id=1, source_target_pairs={{0,1},{1,2},{2,3},{3,4},{4,5},{5,6},{6,7},{7,8},{8,9},{9,10},{10,1... | collective-permute-start | bytes 589832 | tf_op jit(solution)/shard_map/ppermute | solution.py:30
  202.8 7.0 %collective-permute-start.2 = (bf16[1,12,256,32]{2,3,1,0:T(8,128)(2,1)S(1)}, bf16[1,12,256,32]{2,3,1,0:T(8,128)(2,1)S(1)}, u32[]{:S(2)}, u32[]{:S(2)}) collective-permute-start(bf16[1,12,256,32]{2,3,1,0:T(8,128)(2,1)S(1)} %get-tuple-element.83), channel_id=1, source_target_pairs={{1,0},{2,1},{3,2},{4,3},{5,4},{6,5},{7,6},{8,7},{9,8},{10,9},{11,1... | collective-permute-start | bytes 589832 | tf_op jit(solution)/shard_map/ppermute | solution.py:32
  221.4 4.8 %copy-start.5 = (bf16[4,16,64,32]{3,1,2,0:T(8,128)(2,1)S(1)}, bf16[4,16,64,32]{3,1,2,0:T(8,128)(2,1)}, u32[]{:S(2)}) copy-start(bf16[4,16,64,32]{3,1,2,0:T(8,128)(2,1)} %gather_fusion.2) | copy-start | bytes 786436
  222.7 3.5 copy-start.4
  392.9 26.2 %copy-start.1 = (bf16[64,64]{1,0:T(8,128)(2,1)S(1)}, bf16[64,64]{1,0:T(8,128)(2,1)}, u32[]{:S(2)}) copy-start(bf16[64,64]{1,0:T(8,128)(2,1)} %param.12) | copy-start | bytes 24580
where the time goes:
time: 427 us; the launch traced here: 419 us
  local copies, waits for them, and re-layouts  301 us (70%)
  matrix products  53.4 us (13%)
  other arithmetic  31.7 us (7%)
  waiting for transfers between devices  16.8 us (4%)
  starting transfers between devices  15.9 us (4%)
    reshape x1, local copies, waits for them, and re-layouts, first_layer(): paired = image.reshape(rows // 2, 2, cols // 2, 2)  73.3 us
    reshape x2, local copies, waits for them, and re-layouts, one_tile(): flat = products.reshape(TILE, span, TILE_W * width)  62.4 us
    reshape x1, local copies, waits for them, and re-layouts, one_tile(): diagonal = flat.reshape(TILE, span, TILE_W, width + 1)[..., :span]  59.4 us
    dot_general x2, matrix products, first_layer(): jnp.einsum('rck,ko->rco', paired[:, row_phase], weight[row_phase, :, 0, :...  27 us
    reshape x2, local copies, waits for them, and re-layouts, patch_layer(): paired = field.reshape(rows // 2, 2, cols // 2, 2 * chans)  26.6 us
    convert_element_type x1, other arithmetic, correlate(): result = (result * (1.0 / math.sqrt(CF))).astype(jnp.bfloat16)  19.5 us
    dot_general x1, matrix products, one_tile(): jnp.einsum('yxc,ylwc->ylxw', here, lifted, preferred_element_type=jnp.flo...  17.5 us
    convert_element_type x1, local copies, waits for them, and re-layouts, correlate(): result = (result * (1.0 / math.sqrt(CF))).astype(jnp.bfloat16)  16.8 us
  transfers between devices with their start and end apart: 4, of which 3 were waited for; matrix products, arithmetic and copies ran while one was open for 2% of the time, Pallas kernels for 0%

commit v1 on v0

v1 whole, which is shorter than its diff:
```python
import functools
import math

import jax
import jax.numpy as jnp
from jax import lax
from jax.experimental import pallas as pl
from jax.experimental.pallas import tpu as pltpu
from jax.sharding import PartitionSpec as P

REACH = 8
SPAN = 2 * REACH + 1
OFFSETS = SPAN * SPAN
BF = jnp.bfloat16
F32 = jnp.float32

ROWS = 256
CHUNK = 64
BASE = 120
SLACK = 536


def iota(shape, dim):
    return lax.broadcasted_iota(jnp.int32, shape, dim)


def dot(a, b):
    return jnp.dot(a, b, preferred_element_type=F32)


def expand_weights(w1, w2, w3, w4, w5, e1, e2, e3, e4, e5):
    pixel = iota((128, 128), 0)
    column = iota((128, 128), 1) // 32
    for k1 in range(2):
        wide = [
            jnp.broadcast_to(jnp.concatenate([w1[k1, kx].astype(F32)] * 4, axis=1), (128, 128))
            for kx in range(2)
        ]
        for g in range(16):
            phase = pixel - 2 * (4 * g + column)
            block = jnp.where(phase == 0, wide[0], jnp.where(phase == 1, wide[1], 0.0))
            e1[k1 * 128 : k1 * 128 + 128, g * 128 : g * 128 + 128] = block.astype(BF)

    def spread(pieces, rows, outs, count):
        bands = []
        for line in pieces:
            bands.append(
                jnp.concatenate(
                    [jnp.zeros((rows, outs), F32) if p is None else p for p in line], axis=1
                )
            )
        return jnp.concatenate(bands, axis=0).astype(BF)

    for k in range(2):
        pieces = [
            [w2[k, ci % 2].astype(F32) if ci // 2 == co else None for co in range(4)]
            for ci in range(8)
        ]
        e2[k] = spread(pieces, 32, 64, 4)
        pieces = [
            [w3[k, ci % 2].astype(F32) if ci // 2 == co else None for co in range(2)]
            for ci in range(4)
        ]
        e3[k] = spread(pieces, 64, 64, 2)
    e4[...] = spread(
        [[w4[...].astype(F32) if ci == co else None for co in range(4)] for ci in range(4)], 64, 64, 4
    )
    e5[...] = spread(
        [[w5[...].astype(F32) if ci == co else None for co in range(4)] for ci in range(4)], 64, 32, 4
    )


def relu(x):
    return jnp.maximum(x, 0.0).astype(BF)


def encode_chunk(chunk, px, xs, a1, a2, a3, e1, e2, e3, e4, e5, perm):
    for part in range(CHUNK // 32):
        start = pl.multiple_of((chunk * (CHUNK // 32) + part) * 256, 256)
        sorted_rows = dot(perm[...], px[pl.ds(start, 256), :]).astype(BF)
        for k in range(8):
            xs[k // 2, part * 32 : part * 32 + 32, (k % 2) * 128 : (k % 2) * 128 + 128] = sorted_rows[
                k * 32 : k * 32 + 32
            ]
    lhs = xs[...].reshape(4 * CHUNK, 256)
    for j in range(8):
        out = relu(dot(lhs, e1[:, 256 * j : 256 * j + 256]))
        out = out.reshape(2, 2, CHUNK, 256)
        a1[0, j] = out[:, 0].reshape(2 * CHUNK, 256)
        a1[1, j] = out[:, 1].reshape(2 * CHUNK, 256)
    for jj in range(2):
        l0 = a1[0, 4 * jj : 4 * jj + 4].reshape(8 * CHUNK, 256)
        l1 = a1[1, 4 * jj : 4 * jj + 4].reshape(8 * CHUNK, 256)
        out = relu(dot(l0, e2[0]) + dot(l1, e2[1])).reshape(4, 2, CHUNK, 256)
        a2[0, 4 * jj : 4 * jj + 4] = out[:, 0]
        a2[1, 4 * jj : 4 * jj + 4] = out[:, 1]
    l0 = a2[0].reshape(8 * CHUNK, 256)
    l1 = a2[1].reshape(8 * CHUNK, 256)
    out = relu(dot(l0, e3[0]) + dot(l1, e3[1])).reshape(4, 2, CHUNK, 128)
    a3[:, :, 0:128] = out[:, 0]
    a3[:, :, 128:256] = out[:, 1]
    out = relu(dot(a3[...].reshape(4 * CHUNK, 256), e4[...]))
    return dot(out, e5[...]).astype(BF).reshape(4, CHUNK, 128)


def encoder_kernel(px, w1, w2, w3, w4, w5, out, xs, a1, a2, a3, e1, e2, e3, e4, e5, perm):
    expand_weights(w1, w2, w3, w4, w5, e1, e2, e3, e4, e5)
    r = iota((256, 256), 0)
    c = iota((256, 256), 1)
    perm[...] = jnp.where(8 * (r % 32) + r // 32 == c, 1.0, 0.0).astype(BF)

    @pl.loop(0, ROWS // CHUNK)
    def _(chunk):
        done = encode_chunk(chunk, px.at[0], xs, a1, a2, a3, e1, e2, e3, e4, e5, perm)
        out[:, pl.ds(pl.multiple_of(chunk * CHUNK, CHUNK), CHUNK), :] = done


def encode(sections, weights):
    vmem = pl.BlockSpec(memory_space=pltpu.VMEM)
    return pl.pallas_call(
        encoder_kernel,
        out_shape=jax.ShapeDtypeStruct((4, ROWS, 128), BF),
        in_specs=[vmem] * 6,
        out_specs=vmem,
        scratch_shapes=[
            pltpu.VMEM((4, CHUNK, 256), BF),
            pltpu.VMEM((2, 8, 2 * CHUNK, 256), BF),
            pltpu.VMEM((2, 8, CHUNK, 256), BF),
            pltpu.VMEM((4, CHUNK, 256), BF),
            pltpu.VMEM((256, 2048), BF),
            pltpu.VMEM((2, 256, 256), BF),
            pltpu.VMEM((2, 256, 128), BF),
            pltpu.VMEM((256, 256), BF),
            pltpu.VMEM((256, 128), BF),
            pltpu.VMEM((256, 256), BF),
        ],
        compiler_params=pltpu.CompilerParams(vmem_limit_bytes=48 * 2**20),
        name="encode",
    )(sections, *weights)


def correlate_kernel(shift, cur, prior, out, cur32, wide, lhs, rhs, picked, rows):
    wide[0:4] = jnp.zeros((4, 48, 128), F32)
    wide[68:72] = jnp.zeros((4, 48, 128), F32)

    @pl.loop(0, 16)
    def _(i):
        wide[pl.ds(4 + 4 * i, 4)] = prior[pl.ds(4 * i, 4)].astype(F32)
        cur32[pl.ds(4 * i, 4)] = cur[pl.ds(4 * i, 4)].astype(F32)

    lane = iota((8, 128), 1)
    slot = lane // 32
    sub = iota((8, 128), 0)
    lane256 = iota((8, 256), 1)
    block = (lane256 % 32) // 8

    for side in range(2):
        for j in range(4):
            tile = 2 * side + j // 2
            dy = shift[0, 0, tile, 0]
            dx = shift[0, 0, tile, 1]
            if j % 2 == 0:
                @pl.loop(0, 23)
                def _(q):
                    here = wide[16 * tile + q, pl.ds(8 + dy, 32), :]
                    beside = wide[16 * tile + q + 1, pl.ds(8 + dy, 32), :]
                    lhs[0, q] = here.astype(BF)
                    for e in range(1, 4):
                        mixed = jnp.where(iota((32, 128), 1) < 32 * e, beside, here)
                        lhs[e, q] = pltpu.roll(mixed, 128 - 32 * e, 1).astype(BF)

            for half in range(2):
                for u in range(8):
                    y = 8 * half + (u % 4 - j) % 4 + 4 * (u // 4)
                    for m in range(4):
                        q = 32 * side + 8 * j + 2 * m
                        a = jnp.broadcast_to(cur32[q, y : y + 1, :], (8, 128))
                        b = jnp.broadcast_to(cur32[q + 1, y : y + 1, :], (8, 128))
                        a = jnp.where(slot == sub, a, 0.0)
                        b = jnp.where(slot + 4 == sub, b, 0.0)
                        rhs[u * 32 + 8 * m : u * 32 + 8 * m + 8, 0:128] = a
                        rhs[u * 32 + 8 * m : u * 32 + 8 * m + 8, 128:256] = b
                weights = rhs[...].astype(BF)
                for jj in range(8):
                    count = 6 if jj == 0 else 5
                    place = 8 + dx + 32 * (j % 2) + jj
                    e = lax.rem(place, 4)
                    q = lax.div(place, 4)
                    parts = [
                        jnp.concatenate([lhs[e, q + 2 * m], lhs[e, q + 2 * m + 1]], axis=1)
                        for m in range(count)
                    ]
                    product = lax.dot_general(
                        jnp.concatenate(parts, axis=0),
                        weights,
                        (((1,), (1,)), ((), ())),
                        preferred_element_type=F32,
                    ).reshape(count, 4, 8, 256)
                    for ox in range(jj, SPAN, 8):
                        m = ox // 8
                        for i in range(3):
                            piece = product[m + 3, i + half]
                            for b in (2, 1, 0):
                                piece = jnp.where(block == b, product[m + b, i + half], piece)
                            picked[half, j, ox, i] = piece

        for half in range(2):
            @pl.loop(0, SPAN)
            def _(ox):
                for v in range(2):
                    for i in range(3):
                        blocks = [picked[half, j, ox, i, :, 128 * v : 128 * v + 128] for j in range(4)]
                        for k in range(4):
                            merged = blocks[(3 - k) % 4]
                            for u in (2, 1, 0):
                                merged = jnp.where(slot == u, blocks[(u - k) % 4], merged)
                            if k:
                                merged = pltpu.roll(merged, 128 - 32 * k, 1)
                            start = BASE + (8 * i - 4 * v - k) * SPAN + ox
                            rows[4 * v + k, pl.ds(start, 8, stride=SPAN), :] = merged

            @pl.loop(0, 8)
            def _(y):
                done = rows[y, BASE : BASE + OFFSETS, :] * (1.0 / math.sqrt(32))
                out[0, 8 * half + y, :, 128 * side : 128 * side + 128] = done.astype(BF)


def correlate(current, prior, tile_shift):
    vmem = pl.BlockSpec(memory_space=pltpu.VMEM)
    return pl.pallas_call(
        correlate_kernel,
        out_shape=jax.ShapeDtypeStruct((1, 16, OFFSETS, 256), BF),
        in_specs=[pl.BlockSpec(memory_space=pltpu.SMEM), vmem, vmem],
        out_specs=vmem,
        scratch_shapes=[
            pltpu.VMEM((64, 16, 128), F32),
            pltpu.VMEM((72, 48, 128), F32),
            pltpu.VMEM((4, 24, 32, 128), BF),
            pltpu.VMEM((256, 256), F32),
            pltpu.VMEM((2, 4, SPAN, 3, 8, 256), F32),
            pltpu.VMEM((8, SLACK, 128), F32),
        ],
        compiler_params=pltpu.CompilerParams(vmem_limit_bytes=48 * 2**20),
        name="correlate",
    )(tile_shift, current, prior)


def shifted(block, axis, distance):
    devices = range(lax.axis_size(axis))
    route = [(i - distance, i) for i in devices if i - distance in devices]
    return lax.ppermute(block, axis, route)


def local(sections, tile_shift, w_first, w_second, w_third, w_fourth, w_fifth):
    weights = (w_first, w_second, w_third, w_fourth, w_fifth)
    bands = encode(sections, weights)
    current = lax.all_to_all(bands, "tile", split_axis=1, concat_axis=0, tiled=True)
    before = shifted(current, "sec", 1)
    prior = jnp.concatenate([shifted(before, "tile", 1), before, shifted(before, "tile", -1)], axis=1)
    return correlate(current, prior, tile_shift)


def solution(mesh):
    placed = (P("sec", None, "tile"), P("sec", "tile", None, None), P(), P(), P(), P(), P())
    return jax.shard_map(
        local, mesh=mesh, in_specs=placed, out_specs=P("sec", "tile", None, None), check_vma=False
    )
```

time: 427 us -> 77.2 us (0.18)
  the two profiles are of different devices: /device:TPU:33 before, /device:TPU:96 now
where the time goes in v1:
time: 77.2 us; the launch traced here: 76.7 us
  Pallas kernels  27.5 us (36%)
  waiting for transfers between devices  18.2 us (24%)
  blocking collectives  13.7 us (18%)
  starting transfers between devices  10.1 us (13%)
  local copies, waits for them, and re-layouts  7.07 us (9%)
    pallas_call x1, Pallas kernels, correlate(): pl.pallas_call(correlate_kernel, out_shape=jax.ShapeDtypeStruct((1, 16, O...  20.9 us
    ppermute x3, waiting for transfers between devices, shifted(): return lax.ppermute(block, axis, route)  18.2 us
    all_to_all x1, blocking collectives, local(): lax.all_to_all(bands, 'tile', split_axis=1, concat_axis=0, tiled=True)  13.7 us
    ppermute x3, starting transfers between devices, shifted(): return lax.ppermute(block, axis, route)  10.1 us
    pallas_call x1, Pallas kernels, encode(): pl.pallas_call(encoder_kernel, out_shape=jax.ShapeDtypeStruct((4, ROWS, 1...  6.6 us
    unnamed x13, local copies, waits for them, and re-layouts  4.93 us
    pallas_call x1, local copies, waits for them, and re-layouts, correlate(): pl.pallas_call(correlate_kernel, out_shape=jax.ShapeDtypeStruct((1, 16, O...  1.88 us
  transfers between devices with their start and end apart: 3, of which 3 were waited for; matrix products, arithmetic and copies ran while one was open for 0% of the time, Pallas kernels for 0%

profile of v1, /device:TPU:96, one launch (start us, length us, event | category | flops | bytes accessed | tf_op | source)
XLA Modules:
  0.0 76.7 jit_solution(11050406751487041666)
XLA Ops:
  0.0 0.0 copy-start.4
  0.0 0.7 copy.13.w1
  0.7 0.8 %copy.14.w5 = bf16[64,32]{1,0:T(8,128)(2,1)S(1)} copy(bf16[64,32]{0,1:T(8,128)(2,1)} %param.13) | data formatting | bytes 8192 | tf_op args[6]
  1.5 0.0 copy-start
  1.5 1.0 %copy-done = bf16[1,2048,128]{2,1,0:T(8,128)(2,1)S(1)} copy-done((bf16[1,2048,128]{2,1,0:T(8,128)(2,1)S(1)}, bf16[1,2048,128]{2,1,0:T(8,128)(2,1)}, u32[]{:S(2)}) %copy-start) | copy-done | bytes 524312
  2.5 0.0 copy-start.1
  2.5 0.8 %copy-done.1 = bf16[2,2,64,64]{3,2,1,0:T(8,128)(2,1)S(1)} copy-done((bf16[2,2,64,64]{3,2,1,0:T(8,128)(2,1)S(1)}, bf16[2,2,64,64]{3,2,1,0:T(8,128)(2,1)}, u32[]{:S(2)}) %copy-start.1) | copy-done | bytes 32792
  3.4 0.0 copy-start.2
  3.4 0.8 copy-done.2
  4.1 0.0 copy-start.3
  4.1 0.7 copy-done.3
  4.8 6.6 %encode.1 = bf16[4,256,128]{2,1,0:T(8,128)(2,1)S(1)} custom-call(bf16[1,2048,128]{2,1,0:T(8,128)(2,1)S(1)} %copy-done, bf16[2,2,1,32]{3,2,1,0:T(2,128)(2,1)S(1)} %copy.13.w1, bf16[2,2,32,64]{3,2,1,0:T(8,128)(2,1)S(1)} %copy-done.2, bf16[2,2,64,64]{3,2,1,0:T(8,128)(2,1)S(1)} %copy-done.1, bf16[64,64]{1,0:T(8,128)(2,1)S(1)} %copy-done.3, ...), custom_call_target="tpu_custom_call" | custom-call | tf_op jit(solution)/shard_map/encode/pallas_call | solution.py:120
  11.5 0.2 copy.15
  11.7 13.7 %all_to_all.18 = bf16[4,256,128]{2,0,1:T(4,128)(2,1)S(1)} all-to-all(bf16[4,256,128]{2,0,1:T(4,128)(2,1)S(1)} %copy.15), channel_id=1, replica_groups=mesh['sec'=8,'tile'=16] {'tile'}, dimensions={1} | all-to-all | bytes 524288 | tf_op jit(solution)/shard_map/all_to_all | solution.py:257
  25.5 3.4 %collective-permute-start = (bf16[64,16,128]{2,1,0:T(8,128)(2,1)S(1)}, bf16[64,16,128]{2,1,0:T(8,128)(2,1)S(1)}, u32[]{:S(2)}, u32[]{:S(2)}) collective-permute-start(bf16[64,16,128]{2,1,0:T(8,128)(2,1)S(1)} %bitcast.4), channel_id=1, source_target_pairs={{0,16},{16,32},{32,48},{48,64},{64,80},{80,96},{96,112},{1,17},{17... | collective-permute-start | bytes 786440 | tf_op jit(solution)/shard_map/ppermute | solution.py:251
  28.9 8.9 %collective-permute-done = bf16[64,16,128]{2,1,0:T(8,128)(2,1)S(1)} collective-permute-done((bf16[64,16,128]{2,1,0:T(8,128)(2,1)S(1)}, bf16[64,16,128]{2,1,0:T(8,128)(2,1)S(1)}, u32[]{:S(2)}, u32[]{:S(2)}) %collective-permute-start) | collective-permute-done | bytes 262176 | tf_op jit(solution)/shard_map/ppermute | solution.py:251
  37.8 4.8 %collective-permute-start.2 = (bf16[64,16,128]{2,1,0:T(8,128)(2,1)S(1)}, bf16[64,16,128]{2,1,0:T(8,128)(2,1)S(1)}, u32[]{:S(2)}, u32[]{:S(2)}) collective-permute-start(bf16[64,16,128]{2,1,0:T(8,128)(2,1)S(1)} %collective-permute-done), channel_id=1, source_target_pairs={{1,0},{2,1},{3,2},{4,3},{5,4},{6,5},{7,6},{8,7},{9,8},{10,9},{11,1... | collective-permute-start | bytes 786440 | tf_op jit(solution)/shard_map/ppermute | solution.py:251
  42.6 1.9 %collective-permute-start.1 = (bf16[64,16,128]{2,1,0:T(8,128)(2,1)S(1)}, bf16[64,16,128]{2,1,0:T(8,128)(2,1)S(1)}, u32[]{:S(2)}, u32[]{:S(2)}) collective-permute-start(bf16[64,16,128]{2,1,0:T(8,128)(2,1)S(1)} %collective-permute-done), channel_id=1, source_target_pairs={{0,1},{1,2},{2,3},{3,4},{4,5},{5,6},{6,7},{7,8},{8,9},{9,10},{10,1... | collective-permute-start | bytes 786440 | tf_op jit(solution)/shard_map/ppermute | solution.py:251
  44.5 0.0 copy-done.4
  44.5 0.1 copy.17.shift
  44.6 1.8 %collective-permute-done.2 = bf16[64,16,128]{2,1,0:T(8,128)(2,1)S(1)} collective-permute-done((bf16[64,16,128]{2,1,0:T(8,128)(2,1)S(1)}, bf16[64,16,128]{2,1,0:T(8,128)(2,1)S(1)}, u32[]{:S(2)}, u32[]{:S(2)}) %collective-permute-start.2) | collective-permute-done | bytes 262176 | tf_op jit(solution)/shard_map/ppermute | solution.py:251
  46.4 7.4 %collective-permute-done.1 = bf16[64,16,128]{2,1,0:T(8,128)(2,1)S(1)} collective-permute-done((bf16[64,16,128]{2,1,0:T(8,128)(2,1)S(1)}, bf16[64,16,128]{2,1,0:T(8,128)(2,1)S(1)}, u32[]{:S(2)}, u32[]{:S(2)}) %collective-permute-start.1) | collective-permute-done | bytes 262176 | tf_op jit(solution)/shard_map/ppermute | solution.py:251
  53.9 0.1 pad_maximum_fusion.prior
  53.9 20.9 %correlate.1 = bf16[1,16,289,256]{3,2,1,0:T(8,128)(2,1)S(1)} custom-call(s32[1,1,4,2]{3,2,1,0:T(4,128)S(1)} %copy.17.shift, bf16[64,16,128]{2,1,0:T(8,128)(2,1)S(1)} %bitcast.5, bf16[64,48,128]{2,1,0:T(8,128)(2,1)S(1)} %pad_maximum_fusion.prior), custom_call_target="tpu_custom_call" | custom-call | tf_op jit(solution)/shard_map/correlate/pallas_call | solution.py:230
  74.8 1.9 %copy.18 = bf16[1,16,289,256]{3,1,2,0:T(8,128)(2,1)} copy(bf16[1,16,289,256]{3,2,1,0:T(8,128)(2,1)S(1)} %correlate.1) | data formatting | bytes 4734976 | tf_op jit(solution)/shard_map/correlate/pallas_call | solution.py:230
  (1 shorter events, 0.0 us)
Async XLA Ops:
  0.0 44.5 %copy-start.4 = (s32[1,1,4,2]{2,3,1,0:T(2,128)S(1)}, s32[1,1,4,2]{2,3,1,0:T(2,128)}, u32[]{:S(2)}) copy-start(s32[1,1,4,2]{2,3,1,0:T(2,128)} %param.8) | copy-start | bytes 100
  1.5 1.0 %copy-start = (bf16[1,2048,128]{2,1,0:T(8,128)(2,1)S(1)}, bf16[1,2048,128]{2,1,0:T(8,128)(2,1)}, u32[]{:S(2)}) copy-start(bf16[1,2048,128]{2,1,0:T(8,128)(2,1)} %px.1) | copy-start | bytes 1572868
  2.5 0.8 %copy-start.1 = (bf16[2,2,64,64]{3,2,1,0:T(8,128)(2,1)S(1)}, bf16[2,2,64,64]{3,2,1,0:T(8,128)(2,1)}, u32[]{:S(2)}) copy-start(bf16[2,2,64,64]{3,2,1,0:T(8,128)(2,1)} %w3.1) | copy-start | bytes 98308
  3.4 0.8 copy-start.2
  4.1 0.7 copy-start.3
  25.5 12.3 %collective-permute-start = (bf16[64,16,128]{2,1,0:T(8,128)(2,1)S(1)}, bf16[64,16,128]{2,1,0:T(8,128)(2,1)S(1)}, u32[]{:S(2)}, u32[]{:S(2)}) collective-permute-start(bf16[64,16,128]{2,1,0:T(8,128)(2,1)S(1)} %bitcast.4), channel_id=1, source_target_pairs={{0,16},{16,32},{32,48},{48,64},{64,80},{80,96},{96,112},{1,17},{17... | collective-permute-start | bytes 786440 | tf_op jit(solution)/shard_map/ppermute | solution.py:251
  37.8 8.6 %collective-permute-start.2 = (bf16[64,16,128]{2,1,0:T(8,128)(2,1)S(1)}, bf16[64,16,128]{2,1,0:T(8,128)(2,1)S(1)}, u32[]{:S(2)}, u32[]{:S(2)}) collective-permute-start(bf16[64,16,128]{2,1,0:T(8,128)(2,1)S(1)} %collective-permute-done), channel_id=1, source_target_pairs={{1,0},{2,1},{3,2},{4,3},{5,4},{6,5},{7,6},{8,7},{9,8},{10,9},{11,1... | collective-permute-start | bytes 786440 | tf_op jit(solution)/shard_map/ppermute | solution.py:251
  42.6 11.3 %collective-permute-start.1 = (bf16[64,16,128]{2,1,0:T(8,128)(2,1)S(1)}, bf16[64,16,128]{2,1,0:T(8,128)(2,1)S(1)}, u32[]{:S(2)}, u32[]{:S(2)}) collective-permute-start(bf16[64,16,128]{2,1,0:T(8,128)(2,1)S(1)} %collective-permute-done), channel_id=1, source_target_pairs={{0,1},{1,2},{2,3},{3,4},{4,5},{5,6},{6,7},{7,8},{8,9},{9,10},{10,1... | collective-permute-start | bytes 786440 | tf_op jit(solution)/shard_map/ppermute | solution.py:251

commit v2 on v1

--- a/solution.py
+++ b/solution.py
@@ -16,8 +16,7 @@
 
 ROWS = 256
 CHUNK = 64
-BASE = 120
-SLACK = 536
+BASE = 7
 
 
 def iota(shape, dim):
@@ -33,7 +32,7 @@
     column = iota((128, 128), 1) // 32
     for k1 in range(2):
         wide = [
-            jnp.broadcast_to(jnp.concatenate([w1[k1, kx].astype(F32)] * 4, axis=1), (128, 128))
+            jnp.broadcast_to(jnp.concatenate([w1[k1, kx : kx + 1].astype(F32)] * 4, axis=1), (128, 128))
             for kx in range(2)
         ]
         for g in range(16):
@@ -66,7 +65,7 @@
         [[w4[...].astype(F32) if ci == co else None for co in range(4)] for ci in range(4)], 64, 64, 4
     )
     e5[...] = spread(
-        [[w5[...].astype(F32) if ci == co else None for co in range(4)] for ci in range(4)], 64, 32, 4
+        [[jnp.transpose(w5[...].astype(F32)) if ci == co else None for co in range(4)] for ci in range(4)], 64, 32, 4
     )
 
 
@@ -157,8 +156,8 @@
     for side in range(2):
         for j in range(4):
             tile = 2 * side + j // 2
-            dy = shift[0, 0, tile, 0]
-            dx = shift[0, 0, tile, 1]
+            dy = shift[0, tile]
+            dx = shift[1, tile]
             if j % 2 == 0:
                 @pl.loop(0, 23)
                 def _(q):
@@ -216,20 +215,23 @@
                                 merged = jnp.where(slot == u, blocks[(u - k) % 4], merged)
                             if k:
                                 merged = pltpu.roll(merged, 128 - 32 * k, 1)
-                            start = BASE + (8 * i - 4 * v - k) * SPAN + ox
-                            rows[4 * v + k, pl.ds(start, 8, stride=SPAN), :] = merged
-
-            @pl.loop(0, 8)
-            def _(y):
-                done = rows[y, BASE : BASE + OFFSETS, :] * (1.0 / math.sqrt(32))
-                out[0, 8 * half + y, :, 128 * side : 128 * side + 128] = done.astype(BF)
+                            y = 4 * v + k
+                            start = ((BASE + 8 * i - y) * SPAN + ox) * 8 + y
+                            rows[pl.ds(start, 8, stride=8 * SPAN), :] = merged
+
+            @pl.loop(0, SPAN)
+            def _(oy):
+                start = pl.multiple_of((BASE + oy) * SPAN * 8, 8)
+                done = rows[pl.ds(start, SPAN * 8), :] * (1.0 / math.sqrt(32))
+                done = done.astype(BF).reshape(SPAN, 8, 128)
+                out[pl.ds(oy * SPAN, SPAN), 8 * half : 8 * half + 8, 128 * side : 128 * side + 128] = done
 
 
 def correlate(current, prior, tile_shift):
     vmem = pl.BlockSpec(memory_space=pltpu.VMEM)
     return pl.pallas_call(
         correlate_kernel,
-        out_shape=jax.ShapeDtypeStruct((1, 16, OFFSETS, 256), BF),
+        out_shape=jax.ShapeDtypeStruct((OFFSETS, 16, 256), BF),
         in_specs=[pl.BlockSpec(memory_space=pltpu.SMEM), vmem, vmem],
         out_specs=vmem,
         scratch_shapes=[
@@ -238,26 +240,165 @@
             pltpu.VMEM((4, 24, 32, 128), BF),
             pltpu.VMEM((256, 256), F32),
             pltpu.VMEM((2, 4, SPAN, 3, 8, 256), F32),
-            pltpu.VMEM((8, SLACK, 128), F32),
+            pltpu.VMEM(((BASE + 24) * SPAN * 8, 128), F32),
         ],
         compiler_params=pltpu.CompilerParams(vmem_limit_bytes=48 * 2**20),
         name="correlate",
     )(tile_shift, current, prior)
 
 
-def shifted(block, axis, distance):
-    devices = range(lax.axis_size(axis))
-    route = [(i - distance, i) for i in devices if i - distance in devices]
-    return lax.ppermute(block, axis, route)
+def exchange_kernel(bands, cur, prior, send_sem, cur_sem, prior_sem, halo_sem, local_sem):
+    s = lax.axis_index("sec")
+    t = lax.axis_index("tile")
+    secs = lax.axis_size("sec")
+    tiles = lax.axis_size("tile")
+    barrier = pltpu.get_barrier_semaphore()
+
+    def greet(to_s, to_t):
+        pl.semaphore_signal(
+            barrier, inc=1, device_id=(to_s, to_t), device_id_type=pl.DeviceIdType.MESH
+        )
+
+    @pl.loop(1, tiles)
+    def _(k):
+        greet(s, lax.rem(t + k, tiles))
+
+    @pl.when(s > 0)
+    def _():
+        @pl.loop(0, tiles)
+        def _(k):
+            greet(s - 1, lax.rem(t + k, tiles))
+
+    home = pltpu.make_async_copy(
+        bands.at[:, pl.ds(pl.multiple_of(16 * t, 16), 16)], cur.at[pl.ds(4 * t, 4)], local_sem
+    )
+    home.start()
+    blank = jnp.zeros((64, 16, 128), BF)
+
+    @pl.when((s == 0) | (t == 0))
+    def _():
+        prior[:, 0:16] = blank
+
+    @pl.when((s == 0) | (t == tiles - 1))
+    def _():
+        prior[:, 32:48] = blank
+
+    @pl.when(s == 0)
+    def _():
+        prior[:, 16:32] = blank
+
+    @pl.when(s < secs - 1)
+    def _():
+        pl.semaphore_wait(barrier, 2 * tiles - 1)
+
+    @pl.when(s == secs - 1)
+    def _():
+        pl.semaphore_wait(barrier, tiles - 1)
+
+    def block_of(to_t):
+        return bands.at[:, pl.ds(pl.multiple_of(16 * to_t, 16), 16)]
+
+    @pl.loop(0, tiles)
+    def _(k):
+        to_t = lax.rem(t + k, tiles)
+
+        @pl.when(s < secs - 1)
+        def _():
+            pltpu.make_async_remote_copy(
+                src_ref=block_of(to_t),
+                dst_ref=prior.at[pl.ds(4 * t, 4), 16:32],
+                send_sem=send_sem.at[0],
+                recv_sem=prior_sem,
+                device_id=(s + 1, to_t),
+                device_id_type=pl.DeviceIdType.MESH,
+            ).start()
+
+        @pl.when(k > 0)
+        def _():
+            pltpu.make_async_remote_copy(
+                src_ref=block_of(to_t),
+                dst_ref=cur.at[pl.ds(4 * t, 4)],
+                send_sem=send_sem.at[1],
+                recv_sem=cur_sem,
+                device_id=(s, to_t),
+                device_id_type=pl.DeviceIdType.MESH,
+            ).start()
+
+    def halo(to_t, row, sem):
+        return pltpu.make_async_remote_copy(
+            src_ref=prior.at[:, 16:32],
+            dst_ref=prior.at[:, row : row + 16],
+            send_sem=send_sem.at[2 + sem],
+            recv_sem=halo_sem.at[sem],
+            device_id=(s, to_t),
+            device_id_type=pl.DeviceIdType.MESH,
+        )
+
+    def arrive(ref, sem):
+        pltpu.make_async_copy(ref, ref, sem).wait()
+
+    @pl.when(s > 0)
+    def _():
+        arrive(prior.at[:, 16:32], prior_sem)
+
+        @pl.when(t < tiles - 1)
+        def _():
+            halo(t + 1, 0, 0).start()
+
+        @pl.when(t > 0)
+        def _():
+            halo(t - 1, 32, 1).start()
+
+    arrive(cur.at[0:60], cur_sem)
+    home.wait()
+    arrive(bands.at[:, 0:240], send_sem.at[1])
+
+    @pl.when(s < secs - 1)
+    def _():
+        arrive(bands, send_sem.at[0])
+
+    @pl.when(s > 0)
+    def _():
+        @pl.when(t < tiles - 1)
+        def _():
+            halo(t + 1, 0, 0).wait_send()
+            arrive(prior.at[:, 32:48], halo_sem.at[1])
+
+        @pl.when(t > 0)
+        def _():
+            halo(t - 1, 32, 1).wait_send()
+            arrive(prior.at[:, 0:16], halo_sem.at[0])
+
+
+def exchange(bands):
+    vmem = pl.BlockSpec(memory_space=pltpu.VMEM)
+    return pl.pallas_call(
+        exchange_kernel,
+        out_shape=(
+            jax.ShapeDtypeStruct((64, 16, 128), BF),
+            jax.ShapeDtypeStruct((64, 48, 128), BF),
+        ),
+        in_specs=[vmem],
+        out_specs=(vmem, vmem),
+        scratch_shapes=[
+            pltpu.SemaphoreType.DMA((4,)),
+            pltpu.SemaphoreType.DMA,
+            pltpu.SemaphoreType.DMA,
+            pltpu.SemaphoreType.DMA((2,)),
+            pltpu.SemaphoreType.DMA,
+        ],
+        compiler_params=pltpu.CompilerParams(collective_id=0, has_side_effects=True),
+        name="exchange",
+    )(bands)
 
 
 def local(sections, tile_shift, w_first, w_second, w_third, w_fourth, w_fifth):
-    weights = (w_first, w_second, w_third, w_fourth, w_fifth)
+    weights = (w_first.reshape(2, 2, 32), w_second, w_third, w_fourth, w_fifth.T)
     bands = encode(sections, weights)
-    current = lax.all_to_all(bands, "tile", split_axis=1, concat_axis=0, tiled=True)
-    before = shifted(current, "sec", 1)
-    prior = jnp.concatenate([shifted(before, "tile", 1), before, shifted(before, "tile", -1)], axis=1)
-    return correlate(current, prior, tile_shift)
+    current, prior = exchange(bands)
+    shift = jnp.transpose(tile_shift, (0, 1, 3, 2)).reshape(2, 4)
+    found = correlate(current, prior, shift)
+    return jnp.transpose(found[None], (0, 2, 1, 3))
 
 
 def solution(mesh):

time: 77.2 us -> 60.9 us (0.79)
  the two profiles are of different devices: /device:TPU:96 before, /device:TPU:33 now
where the time goes in v2:
time: 60.9 us; the launch traced here: 59.9 us
  Pallas kernels  51.7 us (85%)
  local copies, waits for them, and re-layouts  8.18 us (13%)
    pallas_call x1, Pallas kernels, exchange(): pl.pallas_call(exchange_kernel, out_shape=(jax.ShapeDtypeStruct((64, 16,...  22.7 us
    pallas_call x1, Pallas kernels, correlate(): pl.pallas_call(correlate_kernel, out_shape=jax.ShapeDtypeStruct((OFFSETS,...  22.3 us
    unnamed x20, local copies, waits for them, and re-layouts  8.18 us
    pallas_call x1, Pallas kernels, encode(): pl.pallas_call(encoder_kernel, out_shape=jax.ShapeDtypeStruct((4, ROWS, 1...  6.64 us

profile of v2, /device:TPU:33, one launch (start us, length us, event | category | flops | bytes accessed | tf_op | source)
XLA Modules:
  0.0 59.9 jit_solution(13406078656805669524)
XLA Ops:
  0.0 0.0 copy-start.2
  0.0 1.0 %copy-done.2 = bf16[1,2048,128]{2,1,0:T(8,128)(2,1)S(1)} copy-done((bf16[1,2048,128]{2,1,0:T(8,128)(2,1)S(1)}, bf16[1,2048,128]{2,1,0:T(8,128)(2,1)}, u32[]{:S(2)}) %copy-start.2) | copy-done | bytes 524312
  1.0 0.0 copy-start.4
  1.0 0.8 %copy-done.4 = bf16[2,2,64,64]{3,2,1,0:T(8,128)(2,1)S(1)} copy-done((bf16[2,2,64,64]{3,2,1,0:T(8,128)(2,1)S(1)}, bf16[2,2,64,64]{3,2,1,0:T(8,128)(2,1)}, u32[]{:S(2)}) %copy-start.4) | copy-done | bytes 32792
  1.9 0.0 copy-start.5
  1.9 0.8 %copy-done.5 = bf16[2,2,32,64]{3,2,1,0:T(8,128)(2,1)S(1)} copy-done((bf16[2,2,32,64]{3,2,1,0:T(8,128)(2,1)S(1)}, bf16[2,2,32,64]{3,2,1,0:T(8,128)(2,1)}, u32[]{:S(2)}) %copy-start.5) | copy-done | bytes 16408
  2.6 0.0 copy-start.6
  2.6 0.7 %copy-done.6 = bf16[64,64]{1,0:T(8,128)(2,1)S(1)} copy-done((bf16[64,64]{1,0:T(8,128)(2,1)S(1)}, bf16[64,64]{1,0:T(8,128)(2,1)}, u32[]{:S(2)}) %copy-start.6) | copy-done | bytes 8216
  3.4 0.0 copy-start.7
  3.4 0.7 %copy-done.7 = bf16[64,32]{0,1:T(8,128)(2,1)S(1)} copy-done((bf16[64,32]{0,1:T(8,128)(2,1)S(1)}, bf16[64,32]{0,1:T(8,128)(2,1)}, u32[]{:S(2)}) %copy-start.7) | copy-done | bytes 4120
  4.1 0.0 copy-start.9
  4.1 0.7 %copy-done.9 = bf16[2,2,1,32]{3,1,2,0:T(2,128)(2,1)S(1)} copy-done((bf16[2,2,1,32]{3,1,2,0:T(2,128)(2,1)S(1)}, bf16[2,2,1,32]{3,1,2,0:T(2,128)(2,1)}, u32[]{:S(2)}) %copy-start.9) | copy-done | bytes 280
  4.7 6.6 %encode.1.bands = bf16[4,256,128]{2,1,0:T(8,128)(2,1)S(1)} custom-call(bf16[1,2048,128]{2,1,0:T(8,128)(2,1)S(1)} %copy-done.2, bf16[2,2,32]{2,1,0:T(2,128)(2,1)S(1)} %bitcast.10, bf16[2,2,32,64]{3,2,1,0:T(8,128)(2,1)S(1)} %copy-done.5, bf16[2,2,64,64]{3,2,1,0:T(8,128)(2,1)S(1)} %copy-done.4, bf16[64,64]{1,0:T(8,128)(2,1)S(1)} %copy-done.6, ...), custom_call_target="tpu_custom_call" | custom-call | tf_op jit(solution)/shard_map/encode/pallas_call | solution.py:119
  11.4 0.0 copy-start
  11.4 0.7 %copy-done = bf16[4,256,128]{2,1,0:T(8,128)(2,1)} copy-done((bf16[4,256,128]{2,1,0:T(8,128)(2,1)}, bf16[4,256,128]{2,1,0:T(8,128)(2,1)S(1)}, u32[]{:S(2)}) %copy-start) | copy-done | bytes 262168
  12.1 22.7 %exchange.1 = (bf16[64,16,128]{2,1,0:T(8,128)(2,1)}, bf16[64,48,128]{2,1,0:T(8,128)(2,1)}) custom-call(bf16[4,256,128]{2,1,0:T(8,128)(2,1)} %copy-done), custom_call_target="tpu_custom_call" | custom-call | tf_op jit(solution)/shard_map/exchange/pallas_call | solution.py:375
  34.8 0.0 copy-start.1
  34.9 1.1 %copy-done.1 = bf16[64,48,128]{2,1,0:T(8,128)(2,1)S(1)} copy-done((bf16[64,48,128]{2,1,0:T(8,128)(2,1)S(1)}, bf16[64,48,128]{2,1,0:T(8,128)(2,1)}, u32[]{:S(2)}) %copy-start.1) | copy-done | bytes 786456
  36.0 0.0 copy-start.3
  36.0 0.9 %copy-done.3 = bf16[64,16,128]{2,1,0:T(8,128)(2,1)S(1)} copy-done((bf16[64,16,128]{2,1,0:T(8,128)(2,1)S(1)}, bf16[64,16,128]{2,1,0:T(8,128)(2,1)}, u32[]{:S(2)}) %copy-start.3) | copy-done | bytes 262168
  36.9 0.0 copy-start.8
  36.9 0.7 %copy-done.8 = s32[1,1,4,2]{2,3,1,0:T(2,128)S(1)} copy-done((s32[1,1,4,2]{2,3,1,0:T(2,128)S(1)}, s32[1,1,4,2]{2,3,1,0:T(2,128)}, u32[]{:S(2)}) %copy-start.8) | copy-done | bytes 56
  37.6 22.3 %correlate.1 = bf16[289,16,256]{2,1,0:T(8,128)(2,1)} custom-call(s32[2,4]{1,0:T(2,128)S(1)} %bitcast.9, bf16[64,16,128]{2,1,0:T(8,128)(2,1)S(1)} %copy-done.3, bf16[64,48,128]{2,1,0:T(8,128)(2,1)S(1)} %copy-done.1), custom_call_target="tpu_custom_call" | custom-call | tf_op jit(solution)/shard_map/correlate/pallas_call | solution.py:232
Async XLA Ops:
  0.0 1.0 %copy-start.2 = (bf16[1,2048,128]{2,1,0:T(8,128)(2,1)S(1)}, bf16[1,2048,128]{2,1,0:T(8,128)(2,1)}, u32[]{:S(2)}) copy-start(bf16[1,2048,128]{2,1,0:T(8,128)(2,1)} %px.1) | copy-start | bytes 1572868
  1.0 0.8 %copy-start.4 = (bf16[2,2,64,64]{3,2,1,0:T(8,128)(2,1)S(1)}, bf16[2,2,64,64]{3,2,1,0:T(8,128)(2,1)}, u32[]{:S(2)}) copy-start(bf16[2,2,64,64]{3,2,1,0:T(8,128)(2,1)} %w3.1) | copy-start | bytes 98308
  1.9 0.8 %copy-start.5 = (bf16[2,2,32,64]{3,2,1,0:T(8,128)(2,1)S(1)}, bf16[2,2,32,64]{3,2,1,0:T(8,128)(2,1)}, u32[]{:S(2)}) copy-start(bf16[2,2,32,64]{3,2,1,0:T(8,128)(2,1)} %w2.1) | copy-start | bytes 49156
  2.6 0.7 %copy-start.6 = (bf16[64,64]{1,0:T(8,128)(2,1)S(1)}, bf16[64,64]{1,0:T(8,128)(2,1)}, u32[]{:S(2)}) copy-start(bf16[64,64]{1,0:T(8,128)(2,1)} %w4.1) | copy-start | bytes 24580
  3.4 0.7 %copy-start.7 = (bf16[64,32]{0,1:T(8,128)(2,1)S(1)}, bf16[64,32]{0,1:T(8,128)(2,1)}, u32[]{:S(2)}) copy-start(bf16[64,32]{0,1:T(8,128)(2,1)} %param.13) | copy-start | bytes 12292
  4.1 0.7 %copy-start.9 = (bf16[2,2,1,32]{3,1,2,0:T(2,128)(2,1)S(1)}, bf16[2,2,1,32]{3,1,2,0:T(2,128)(2,1)}, u32[]{:S(2)}) copy-start(bf16[2,2,1,32]{3,1,2,0:T(2,128)(2,1)} %param.9) | copy-start | bytes 772
  11.4 0.7 %copy-start = (bf16[4,256,128]{2,1,0:T(8,128)(2,1)}, bf16[4,256,128]{2,1,0:T(8,128)(2,1)S(1)}, u32[]{:S(2)}) copy-start(bf16[4,256,128]{2,1,0:T(8,128)(2,1)S(1)} %encode.1.bands) | copy-start | bytes 786436
  34.8 1.1 %copy-start.1 = (bf16[64,48,128]{2,1,0:T(8,128)(2,1)S(1)}, bf16[64,48,128]{2,1,0:T(8,128)(2,1)}, u32[]{:S(2)}) copy-start(bf16[64,48,128]{2,1,0:T(8,128)(2,1)} %get-tuple-element.8.prior) | copy-start | bytes 2359300
  36.0 0.9 %copy-start.3 = (bf16[64,16,128]{2,1,0:T(8,128)(2,1)S(1)}, bf16[64,16,128]{2,1,0:T(8,128)(2,1)}, u32[]{:S(2)}) copy-start(bf16[64,16,128]{2,1,0:T(8,128)(2,1)} %get-tuple-element.7.cur) | copy-start | bytes 786436
  36.9 0.7 %copy-start.8 = (s32[1,1,4,2]{2,3,1,0:T(2,128)S(1)}, s32[1,1,4,2]{2,3,1,0:T(2,128)}, u32[]{:S(2)}) copy-start(s32[1,1,4,2]{2,3,1,0:T(2,128)} %param.8) | copy-start | bytes 100

commit v3 on v1

--- a/solution.py
+++ b/solution.py
@@ -16,8 +16,8 @@
 
 ROWS = 256
 CHUNK = 64
-BASE = 120
-SLACK = 536
+LIMIT = 60 * 2**20
+BASE = 7
 
 
 def iota(shape, dim):
@@ -33,7 +33,7 @@
     column = iota((128, 128), 1) // 32
     for k1 in range(2):
         wide = [
-            jnp.broadcast_to(jnp.concatenate([w1[k1, kx].astype(F32)] * 4, axis=1), (128, 128))
+            jnp.broadcast_to(jnp.concatenate([w1[k1, kx : kx + 1].astype(F32)] * 4, axis=1), (128, 128))
             for kx in range(2)
         ]
         for g in range(16):
@@ -66,7 +66,7 @@
         [[w4[...].astype(F32) if ci == co else None for co in range(4)] for ci in range(4)], 64, 64, 4
     )
     e5[...] = spread(
-        [[w5[...].astype(F32) if ci == co else None for co in range(4)] for ci in range(4)], 64, 32, 4
+        [[jnp.transpose(w5[...].astype(F32)) if ci == co else None for co in range(4)] for ci in range(4)], 64, 32, 4
     )
 
 
@@ -74,10 +74,9 @@
     return jnp.maximum(x, 0.0).astype(BF)
 
 
-def encode_chunk(chunk, px, xs, a1, a2, a3, e1, e2, e3, e4, e5, perm):
+def encode_chunk(px, xs, a1, a2, a3, e1, e2, e3, e4, e5, perm):
     for part in range(CHUNK // 32):
-        start = pl.multiple_of((chunk * (CHUNK // 32) + part) * 256, 256)
-        sorted_rows = dot(perm[...], px[pl.ds(start, 256), :]).astype(BF)
+        sorted_rows = dot(perm[...], px[part * 256 : part * 256 + 256, :]).astype(BF)
         for k in range(8):
             xs[k // 2, part * 32 : part * 32 + 32, (k % 2) * 128 : (k % 2) * 128 + 128] = sorted_rows[
                 k * 32 : k * 32 + 32
@@ -103,26 +102,181 @@
     return dot(out, e5[...]).astype(BF).reshape(4, CHUNK, 128)
 
 
-def encoder_kernel(px, w1, w2, w3, w4, w5, out, xs, a1, a2, a3, e1, e2, e3, e4, e5, perm):
-    expand_weights(w1, w2, w3, w4, w5, e1, e2, e3, e4, e5)
+def share_kernel(
+    px_hbm, w1_hbm, w2_hbm, w3_hbm, w4_hbm, w5_hbm, cur, prior,
+    px, w1, w2, w3, w4, w5, bands, xs, a1, a2, a3, e1, e2, e3, e4, e5, perm,
+    load_sem, px_sem, send_sem, cur_sem, prior_sem, halo_send, halo_recv, home_sem,
+):
+    s = lax.axis_index("sec")
+    t = lax.axis_index("tile")
+    secs = lax.axis_size("sec")
+    tiles = lax.axis_size("tile")
+    group = lax.rem(t, 4)
+    member = lax.div(t, 4)
+    chunks = ROWS // CHUNK
+    pixels = 8 * CHUNK
+
+    loads = [
+        pltpu.make_async_copy(a, b, load_sem.at[i])
+        for i, (a, b) in enumerate(
+            [(w1_hbm, w1), (w2_hbm, w2), (w3_hbm, w3), (w4_hbm, w4), (w5_hbm, w5)]
+        )
+    ]
+    for load in loads:
+        load.start()
+
+    def fetch(phase):
+        chunk = lax.rem(t + phase, chunks)
+        return pltpu.make_async_copy(
+            px_hbm.at[0, pl.ds(pl.multiple_of(chunk * pixels, pixels), pixels)],
+            px.at[phase],
+            px_sem.at[phase],
+        )
+
+    for phase in range(chunks):
+        fetch(phase).start()
+
+    barrier = pltpu.get_barrier_semaphore()
+
+    def greet(to_s, to_t):
+        pl.semaphore_signal(
+            barrier, inc=1, device_id=(to_s, to_t), device_id_type=pl.DeviceIdType.MESH
+        )
+
+    @pl.loop(1, tiles)
+    def _(k):
+        greet(s, lax.rem(t + k, tiles))
+
+    @pl.when(s > 0)
+    def _():
+        @pl.loop(0, tiles)
+        def _(k):
+            greet(s - 1, lax.rem(t + k, tiles))
+
     r = iota((256, 256), 0)
     c = iota((256, 256), 1)
     perm[...] = jnp.where(8 * (r % 32) + r // 32 == c, 1.0, 0.0).astype(BF)
-
-    @pl.loop(0, ROWS // CHUNK)
-    def _(chunk):
-        done = encode_chunk(chunk, px.at[0], xs, a1, a2, a3, e1, e2, e3, e4, e5, perm)
-        out[:, pl.ds(pl.multiple_of(chunk * CHUNK, CHUNK), CHUNK), :] = done
-
-
-def encode(sections, weights):
-    vmem = pl.BlockSpec(memory_space=pltpu.VMEM)
+    for load in loads:
+        load.wait()
+    expand_weights(w1, w2, w3, w4, w5, e1, e2, e3, e4, e5)
+
+    def band_of(to_t):
+        return bands.at[:, pl.ds(pl.multiple_of(16 * to_t, 16), 16)]
+
+    home = pltpu.make_async_copy(band_of(t), cur.at[member, group], home_sem)
+
+    @pl.loop(0, chunks)
+    def _(phase):
+        chunk = lax.rem(t + phase, chunks)
+        fetch(phase).wait()
+        done = encode_chunk(px.at[phase], xs, a1, a2, a3, e1, e2, e3, e4, e5, perm)
+        bands[:, pl.ds(pl.multiple_of(chunk * CHUNK, CHUNK), CHUNK), :] = done
+
+        @pl.when(phase == 0)
+        def _():
+            @pl.when(s < secs - 1)
+            def _():
+                pl.semaphore_wait(barrier, 2 * tiles - 1)
+
+            @pl.when(s == secs - 1)
+            def _():
+                pl.semaphore_wait(barrier, tiles - 1)
+
+        @pl.loop(0, CHUNK // 16)
+        def _(k):
+            to_t = chunk * (CHUNK // 16) + lax.rem(k + member, CHUNK // 16)
+
+            @pl.when(s < secs - 1)
+            def _():
+                pltpu.make_async_remote_copy(
+                    src_ref=band_of(to_t),
+                    dst_ref=prior.at[member, group, :, 16:32],
+                    send_sem=send_sem.at[0],
+                    recv_sem=prior_sem.at[group],
+                    device_id=(s + 1, to_t),
+                    device_id_type=pl.DeviceIdType.MESH,
+                ).start()
+
+            @pl.when(to_t != t)
+            def _():
+                pltpu.make_async_remote_copy(
+                    src_ref=band_of(to_t),
+                    dst_ref=cur.at[member, group],
+                    send_sem=send_sem.at[1],
+                    recv_sem=cur_sem.at[0],
+                    device_id=(s, to_t),
+                    device_id_type=pl.DeviceIdType.MESH,
+                ).start()
+
+            @pl.when(to_t == t)
+            def _():
+                home.start()
+
+    def halo(to_t, row, side, g):
+        return pltpu.make_async_remote_copy(
+            src_ref=prior.at[:, g, :, 16:32],
+            dst_ref=prior.at[:, g, :, row : row + 16],
+            send_sem=halo_send.at[side, g],
+            recv_sem=halo_recv.at[side, g],
+            device_id=(s, to_t),
+            device_id_type=pl.DeviceIdType.MESH,
+        )
+
+    def arrive(ref, sem):
+        pltpu.make_async_copy(ref, ref, sem).wait()
+
+    @pl.when(s > 0)
+    def _():
+        @pl.loop(0, 4)
+        def _(k):
+            g = lax.rem(member - k + 4, 4)
+            arrive(prior.at[:, g, :, 16:32], prior_sem.at[g])
+
+            @pl.when(t < tiles - 1)
+            def _():
+                halo(t + 1, 0, 0, g).start()
+
+            @pl.when(t > 0)
+            def _():
+                halo(t - 1, 32, 1, g).start()
+
+    home.wait()
+    arrive(bands.at[:, 0:240], cur_sem.at[0])
+    arrive(bands.at[:, 0:240], send_sem.at[1])
+
+    @pl.when(s < secs - 1)
+    def _():
+        arrive(bands, send_sem.at[0])
+
+    @pl.when(s > 0)
+    def _():
+        @pl.loop(0, 4)
+        def _(g):
+            @pl.when(t < tiles - 1)
+            def _():
+                halo(t + 1, 0, 0, g).wait_send()
+                arrive(prior.at[:, g, :, 32:48], halo_recv.at[1, g])
+
+            @pl.when(t > 0)
+            def _():
+                halo(t - 1, 32, 1, g).wait_send()
+                arrive(prior.at[:, g, :, 0:16], halo_recv.at[0, g])
+
+
+def share(sections, weights):
+    hbm = pl.BlockSpec(memory_space=pltpu.HBM)
     return pl.pallas_call(
-        encoder_kernel,
-        out_shape=jax.ShapeDtypeStruct((4, ROWS, 128), BF),
-        in_specs=[vmem] * 6,
-        out_specs=vmem,
+        share_kernel,
+        out_shape=(
+            jax.ShapeDtypeStruct((4, 4, 4, 16, 128), BF),
+            jax.ShapeDtypeStruct((4, 4, 4, 48, 128), BF),
+        ),
+        in_specs=[hbm] * 6,
+        out_specs=(hbm, hbm),
         scratch_shapes=[
+            pltpu.VMEM((ROWS // CHUNK, 8 * CHUNK, 128), BF),
+            *[pltpu.VMEM(w.shape, BF) for w in weights],
+            pltpu.VMEM((4, ROWS, 128), BF),
             pltpu.VMEM((4, CHUNK, 256), BF),
             pltpu.VMEM((2, 8, 2 * CHUNK, 256), BF),
             pltpu.VMEM((2, 8, CHUNK, 256), BF),
@@ -133,20 +287,53 @@
             pltpu.VMEM((256, 256), BF),
             pltpu.VMEM((256, 128), BF),
             pltpu.VMEM((256, 256), BF),
+            pltpu.SemaphoreType.DMA((5,)),
+            pltpu.SemaphoreType.DMA((ROWS // CHUNK,)),
+            pltpu.SemaphoreType.DMA((2,)),
+            pltpu.SemaphoreType.DMA((1,)),
+            pltpu.SemaphoreType.DMA((4,)),
+            pltpu.SemaphoreType.DMA((2, 4)),
+            pltpu.SemaphoreType.DMA((2, 4)),
+            pltpu.SemaphoreType.DMA,
         ],
-        compiler_params=pltpu.CompilerParams(vmem_limit_bytes=48 * 2**20),
-        name="encode",
+        compiler_params=pltpu.CompilerParams(
+            vmem_limit_bytes=LIMIT, collective_id=0, has_side_effects=True
+        ),
+        name="share",
     )(sections, *weights)
 
 
-def correlate_kernel(shift, cur, prior, out, cur32, wide, lhs, rhs, picked, rows):
+def correlate_kernel(
+    shift, cur_hbm, prior_hbm, out_hbm, cur, prior, cur32, wide, lhs, rhs, picked, rows, out, in_sem, out_sem
+):
+    s = lax.axis_index("sec")
+    t = lax.axis_index("tile")
+    loads = []
+    for i in range(4):
+        near = pl.ds(16 * i, 16)
+        loads.append(
+            (
+                pltpu.make_async_copy(prior_hbm.at[near], prior.at[near], in_sem.at[0, i]),
+                pltpu.make_async_copy(cur_hbm.at[near], cur.at[near], in_sem.at[1, i]),
+            )
+        )
+    for pair in loads:
+        for load in pair:
+            load.start()
     wide[0:4] = jnp.zeros((4, 48, 128), F32)
     wide[68:72] = jnp.zeros((4, 48, 128), F32)
 
-    @pl.loop(0, 16)
-    def _(i):
-        wide[pl.ds(4 + 4 * i, 4)] = prior[pl.ds(4 * i, 4)].astype(F32)
-        cur32[pl.ds(4 * i, 4)] = cur[pl.ds(4 * i, 4)].astype(F32)
+    row = iota((1, 48, 128), 1)
+    first = jnp.where(t == 0, 16, 0)
+    last = jnp.where(t == lax.axis_size("tile") - 1, 32, 48)
+    last = jnp.where(s == 0, 0, last)
+    inside = (row >= first) & (row < last)
+    for i in range(16):
+        if i % 4 == 0:
+            for load in loads[i // 4]:
+                load.wait()
+        wide[4 + 4 * i : 8 + 4 * i] = jnp.where(inside, prior[4 * i : 4 * i + 4].astype(F32), 0.0)
+        cur32[4 * i : 4 * i + 4] = cur[4 * i : 4 * i + 4].astype(F32)
 
     lane = iota((8, 128), 1)
     slot = lane // 32
@@ -154,13 +341,14 @@
     lane256 = iota((8, 256), 1)
     block = (lane256 % 32) // 8
 
+    sends = []
     for side in range(2):
         for j in range(4):
             tile = 2 * side + j // 2
-            dy = shift[0, 0, tile, 0]
-            dx = shift[0, 0, tile, 1]
+            dy = shift[0, tile]
+            dx = shift[1, tile]
             if j % 2 == 0:
-                @pl.loop(0, 23)
+                @pl.loop(0, 23, unroll=True)
                 def _(q):
                     here = wide[16 * tile + q, pl.ds(8 + dy, 32), :]
                     beside = wide[16 * tile + q + 1, pl.ds(8 + dy, 32), :]
@@ -205,7 +393,7 @@
                             picked[half, j, ox, i] = piece
 
         for half in range(2):
-            @pl.loop(0, SPAN)
+            @pl.loop(0, SPAN, unroll=True)
             def _(ox):
                 for v in range(2):
                     for i in range(3):
@@ -216,48 +404,60 @@
                                 merged = jnp.where(slot == u, blocks[(u - k) % 4], merged)
                             if k:
                                 merged = pltpu.roll(merged, 128 - 32 * k, 1)
-                            start = BASE + (8 * i - 4 * v - k) * SPAN + ox
-                            rows[4 * v + k, pl.ds(start, 8, stride=SPAN), :] = merged
-
-            @pl.loop(0, 8)
-            def _(y):
-                done = rows[y, BASE : BASE + OFFSETS, :] * (1.0 / math.sqrt(32))
-                out[0, 8 * half + y, :, 128 * side : 128 * side + 128] = done.astype(BF)
+                            y = 4 * v + k
+                            start = ((BASE + 8 * i - y) * SPAN + ox) * 8 + y
+                            rows[pl.ds(start, 8, stride=8 * SPAN), :] = merged
+
+            @pl.loop(0, SPAN, unroll=True)
+            def _(oy):
+                start = pl.multiple_of((BASE + oy) * SPAN * 8, 8)
+                done = rows[pl.ds(start, SPAN * 8), :] * (1.0 / math.sqrt(32))
+                done = done.astype(BF).reshape(SPAN, 8, 128)
+                out[side, pl.ds(oy * SPAN, SPAN), 8 * half : 8 * half + 8, :] = done
+
+        sends.append(
+            pltpu.make_async_copy(
+                out.at[side], out_hbm.at[:, :, pl.ds(128 * side, 128)], out_sem.at[side]
+            )
+        )
+        sends[-1].start()
+    for send in sends:
+        send.wait()
 
 
 def correlate(current, prior, tile_shift):
-    vmem = pl.BlockSpec(memory_space=pltpu.VMEM)
+    hbm = pl.BlockSpec(memory_space=pltpu.HBM)
     return pl.pallas_call(
         correlate_kernel,
-        out_shape=jax.ShapeDtypeStruct((1, 16, OFFSETS, 256), BF),
-        in_specs=[pl.BlockSpec(memory_space=pltpu.SMEM), vmem, vmem],
-        out_specs=vmem,
+        out_shape=jax.ShapeDtypeStruct((OFFSETS, 16, 256), BF),
+        in_specs=[pl.BlockSpec(memory_space=pltpu.SMEM), hbm, hbm],
+        out_specs=hbm,
         scratch_shapes=[
+            pltpu.VMEM((64, 16, 128), BF),
+            pltpu.VMEM((64, 48, 128), BF),
             pltpu.VMEM((64, 16, 128), F32),
             pltpu.VMEM((72, 48, 128), F32),
             pltpu.VMEM((4, 24, 32, 128), BF),
             pltpu.VMEM((256, 256), F32),
             pltpu.VMEM((2, 4, SPAN, 3, 8, 256), F32),
-            pltpu.VMEM((8, SLACK, 128), F32),
+            pltpu.VMEM(((BASE + 24) * SPAN * 8, 128), F32),
+            pltpu.VMEM((2, OFFSETS, 16, 128), BF),
+            pltpu.SemaphoreType.DMA((2, 4)),
+            pltpu.SemaphoreType.DMA((2,)),
         ],
-        compiler_params=pltpu.CompilerParams(vmem_limit_bytes=48 * 2**20),
+        compiler_params=pltpu.CompilerParams(vmem_limit_bytes=LIMIT),
         name="correlate",
     )(tile_shift, current, prior)
 
 
-def shifted(block, axis, distance):
-    devices = range(lax.axis_size(axis))
-    route = [(i - distance, i) for i in devices if i - distance in devices]
-    return lax.ppermute(block, axis, route)
-
-
 def local(sections, tile_shift, w_first, w_second, w_third, w_fourth, w_fifth):
-    weights = (w_first, w_second, w_third, w_fourth, w_fifth)
-    bands = encode(sections, weights)
-    current = lax.all_to_all(bands, "tile", split_axis=1, concat_axis=0, tiled=True)
-    before = shifted(current, "sec", 1)
-    prior = jnp.concatenate([shifted(before, "tile", 1), before, shifted(before, "tile", -1)], axis=1)
-    return correlate(current, prior, tile_shift)
+    weights = (w_first.reshape(2, 2, 32), w_second, w_third, w_fourth, w_fifth.T)
+    current, prior = share(sections, weights)
+    current = current.reshape(64, 16, 128)
+    prior = prior.reshape(64, 48, 128)
+    shift = jnp.transpose(tile_shift, (0, 1, 3, 2)).reshape(2, 4)
+    found = correlate(current, prior, shift)
+    return jnp.transpose(found[None], (0, 2, 1, 3))
 
 
 def solution(mesh):

time: 77.2 us -> 32 us (0.41)
  the two profiles are of different devices: /device:TPU:96 before, /device:TPU:57 now
where the time goes in v3:
time: 32 us; the launch traced here: 31.8 us
  Pallas kernels  31.8 us (99%)
    pallas_call x1, Pallas kernels, share(): pl.pallas_call(share_kernel, out_shape=(jax.ShapeDtypeStruct((4, 4, 4, 16...  21.5 us
    pallas_call x1, Pallas kernels, correlate(): pl.pallas_call(correlate_kernel, out_shape=jax.ShapeDtypeStruct((OFFSETS,...  10.3 us

profile of v3, /device:TPU:57, one launch (start us, length us, event | category | flops | bytes accessed | tf_op | source)
XLA Modules:
  0.0 31.8 jit_solution(2351344001417615493)
XLA Ops:
  0.0 21.5 %share.1 = (bf16[4,4,4,16,128]{4,3,2,1,0:T(8,128)(2,1)}, bf16[4,4,4,48,128]{4,3,2,1,0:T(8,128)(2,1)}) custom-call(bf16[1,2048,128]{2,1,0:T(8,128)(2,1)} %px_hbm.1, bf16[2,2,32]{2,1,0:T(2,128)(2,1)} %bitcast.14, bf16[2,2,32,64]{3,2,1,0:T(8,128)(2,1)} %w2_hbm.1, bf16[2,2,64,64]{3,2,1,0:T(8,128)(2,1)} %w3_hbm.1, bf16[64,64]{1,0:T(8,128)(2,1)} %w4_hbm.1, ...), custom_call_target="tpu_custom_call" | custom-call | tf_op jit(solution)/shard_map/share/pallas_call | solution.py:268
  21.5 10.3 %correlate.1 = bf16[289,16,256]{2,1,0:T(8,128)(2,1)} custom-call(s32[2,4]{1,0:T(2,128)} %bitcast.13, bf16[64,16,128]{2,1,0:T(8,128)(2,1)} %bitcast.11, bf16[64,48,128]{2,1,0:T(8,128)(2,1)} %bitcast.10), custom_call_target="tpu_custom_call" | custom-call | tf_op jit(solution)/shard_map/correlate/pallas_call | solution.py:430

commit v4 on v3

v4 whole, which is shorter than its diff:
```python
import functools
import math

import jax
import jax.numpy as jnp
from jax import lax
from jax.experimental import pallas as pl
from jax.experimental.pallas import tpu as pltpu
from jax.sharding import PartitionSpec as P

REACH = 8
SPAN = 2 * REACH + 1
OFFSETS = SPAN * SPAN
BF = jnp.bfloat16
F32 = jnp.float32

ROWS = 256
CHUNK = 64
LIMIT = 60 * 2**20
SENT = (6, 12, 17)
GROUP = 8
HELD = 1
BASE = 7


def iota(shape, dim):
    return lax.broadcasted_iota(jnp.int32, shape, dim)


def dot(a, b):
    return jnp.dot(a, b, preferred_element_type=F32)


def expand_weights(w1, w2, w3, w4, w5, e1, e2, e3, e4, e5):
    pixel = iota((128, 128), 0)
    column = iota((128, 128), 1) // 32
    for k1 in range(2):
        wide = [
            jnp.broadcast_to(jnp.concatenate([w1[k1, kx : kx + 1].astype(F32)] * 4, axis=1), (128, 128))
            for kx in range(2)
        ]
        for g in range(16):
            phase = pixel - 2 * (4 * g + column)
            block = jnp.where(phase == 0, wide[0], jnp.where(phase == 1, wide[1], 0.0))
            e1[k1 * 128 : k1 * 128 + 128, g * 128 : g * 128 + 128] = block.astype(BF)

    def spread(pieces, rows, outs, count):
        bands = []
        for line in pieces:
            bands.append(
                jnp.concatenate(
                    [jnp.zeros((rows, outs), F32) if p is None else p for p in line], axis=1
                )
            )
        return jnp.concatenate(bands, axis=0).astype(BF)

    for k in range(2):
        pieces = [
            [w2[k, ci % 2].astype(F32) if ci // 2 == co else None for co in range(4)]
            for ci in range(8)
        ]
        e2[256 * k : 256 * k + 256] = spread(pieces, 32, 64, 4)
        pieces = [
            [w3[k, ci % 2].astype(F32) if ci // 2 == co else None for co in range(2)]
            for ci in range(4)
        ]
        e3[256 * k : 256 * k + 256] = spread(pieces, 64, 64, 2)
    e4[...] = spread(
        [[w4[...].astype(F32) if ci == co else None for co in range(4)] for ci in range(4)], 64, 64, 4
    )
    e5[...] = spread(
        [[jnp.transpose(w5[...].astype(F32)) if ci == co else None for co in range(4)] for ci in range(4)], 64, 32, 4
    )


def relu(x):
    return jnp.maximum(x, 0.0).astype(BF)


def encode_chunk(px, xs, a1, a2, a3, e1, e2, e3, e4, e5, perm):
    for part in range(CHUNK // 32):
        sorted_rows = dot(perm[...], px[part * 256 : part * 256 + 256, :]).astype(BF)
        for k in range(8):
            xs[k // 2, part * 32 : part * 32 + 32, (k % 2) * 128 : (k % 2) * 128 + 128] = sorted_rows[
                k * 32 : k * 32 + 32
            ]
    lhs = xs[...].reshape(4 * CHUNK, 256)
    for j in range(4):
        out = relu(dot(lhs, e1[:, 512 * j : 512 * j + 512]))
        out = out.reshape(2, 2, CHUNK, 512)
        for half in range(2):
            for k2 in range(2):
                a1[2 * j + half, :, 256 * k2 : 256 * k2 + 256] = out[
                    :, k2, :, 256 * half : 256 * half + 256
                ].reshape(2 * CHUNK, 256)
    for j in range(2):
        out = relu(dot(a1[4 * j : 4 * j + 4].reshape(8 * CHUNK, 512), e2[...]))
        out = out.reshape(4, 2, CHUNK, 256)
        for k3 in range(2):
            a2[4 * j : 4 * j + 4, :, 256 * k3 : 256 * k3 + 256] = out[:, k3]
    out = relu(dot(a2[...].reshape(8 * CHUNK, 512), e3[...])).reshape(4, 2, CHUNK, 128)
    a3[:, :, 0:128] = out[:, 0]
    a3[:, :, 128:256] = out[:, 1]
    out = relu(dot(a3[...].reshape(4 * CHUNK, 256), e4[...]))
    return dot(out, e5[...]).astype(BF).reshape(4, CHUNK, 128)


def share_kernel(
    px_hbm, w1_hbm, w2_hbm, w3_hbm, w4_hbm, w5_hbm, cur, prior,
    px, w1, w2, w3, w4, w5, bands, xs, a1, a2, a3, e1, e2, e3, e4, e5, perm,
    load_sem, px_sem, send_sem, cur_sem, prior_sem, halo_send, halo_recv, home_sem,
):
    s = lax.axis_index("sec")
    t = lax.axis_index("tile")
    secs = lax.axis_size("sec")
    tiles = lax.axis_size("tile")
    group = lax.rem(t, 4)
    member = lax.div(t, 4)
    chunks = ROWS // CHUNK
    pixels = 8 * CHUNK

    def chunk_at(phase):
        flip = jnp.int32(chunks - 1) - phase
        high = lax.rem(lax.div(member, 2) + lax.div(flip, 2), 2)
        return 2 * high + lax.rem(member + flip, 2)


    barrier = pltpu.get_barrier_semaphore()

    def greet(to_s, to_t):
        pl.semaphore_signal(
            barrier, inc=1, device_id=(to_s, to_t), device_id_type=pl.DeviceIdType.MESH
        )

    @pl.loop(1, tiles)
    def _(k):
        greet(s, lax.rem(t + k, tiles))

    @pl.when(s > 0)
    def _():
        @pl.loop(0, tiles)
        def _(k):
            greet(s - 1, lax.rem(t + k, tiles))

    loads = [
        pltpu.make_async_copy(a, b, load_sem.at[i])
        for i, (a, b) in enumerate(
            [(w1_hbm, w1), (w2_hbm, w2), (w3_hbm, w3), (w4_hbm, w4), (w5_hbm, w5)]
        )
    ]
    for load in loads:
        load.start()

    def fetch(phase):
        chunk = chunk_at(phase)
        return pltpu.make_async_copy(
            px_hbm.at[0, pl.ds(pl.multiple_of(chunk * pixels, pixels), pixels)],
            px.at[phase],
            px_sem.at[phase],
        )

    for phase in range(chunks):
        fetch(phase).start()

    r = iota((256, 256), 0)
    c = iota((256, 256), 1)
    perm[...] = jnp.where(8 * (r % 32) + r // 32 == c, 1.0, 0.0).astype(BF)
    for load in loads:
        load.wait()
    expand_weights(w1, w2, w3, w4, w5, e1, e2, e3, e4, e5)

    def band_of(to_t):
        return bands.at[:, pl.ds(pl.multiple_of(16 * to_t, 16), 16)]

    home = pltpu.make_async_copy(band_of(t), cur.at[member, group], home_sem)

    def encode_phase(phase):
        chunk = chunk_at(phase)
        fetch(phase).wait()
        done = encode_chunk(px.at[phase], xs, a1, a2, a3, e1, e2, e3, e4, e5, perm)
        bands[:, pl.ds(pl.multiple_of(chunk * CHUNK, CHUNK), CHUNK), :] = done

    def send_phase(phase):
        chunk = chunk_at(phase)

        def push(to_t, to_s, by, dst, sem):
            pltpu.make_async_remote_copy(
                src_ref=band_of(to_t),
                dst_ref=dst,
                send_sem=send_sem.at[by],
                recv_sem=sem,
                device_id=to_s,
                device_id_type=pl.DeviceIdType.MESH,
            ).start()

        @pl.when(s < secs - 1)
        def _():
            @pl.loop(0, CHUNK // 16)
            def _(k):
                to_t = chunk * (CHUNK // 16) + lax.rem(k + member, CHUNK // 16)
                push(to_t, (s + 1, to_t), 0, prior.at[member, group, :, 16:32], prior_sem.at[member])

                @pl.when(to_t == tiles // 2 - 1)
                def _():
                    push(to_t, (s + 1, to_t + 1), 2, prior.at[member, group, :, 0:16], halo_recv.at[0, member])

                @pl.when(to_t == tiles // 2)
                def _():
                    push(to_t, (s + 1, to_t - 1), 2, prior.at[member, group, :, 32:48], halo_recv.at[1, member])

        @pl.loop(0, CHUNK // 16)
        def _(k):
            to_t = chunk * (CHUNK // 16) + lax.rem(k + member, CHUNK // 16)

            @pl.when(to_t != t)
            def _():
                push(to_t, (s, to_t), 1, cur.at[member, group], cur_sem.at[0])

            @pl.when(to_t == t)
            def _():
                home.start()

    @pl.loop(0, chunks)
    def _(phase):
        encode_phase(phase)

        @pl.when(phase == HELD - 1)
        def _():
            @pl.when(s < secs - 1)
            def _():
                pl.semaphore_wait(barrier, 2 * tiles - 1)

            @pl.when(s == secs - 1)
            def _():
                pl.semaphore_wait(barrier, tiles - 1)

            @pl.loop(0, HELD)
            def _(before):
                send_phase(before)

        @pl.when(phase >= HELD)
        def _():
            send_phase(phase)

    def halo(to_t, row, side, g):
        return pltpu.make_async_remote_copy(
            src_ref=prior.at[g, :, :, 16:32],
            dst_ref=prior.at[g, :, :, row : row + 16],
            send_sem=halo_send.at[side, g],
            recv_sem=halo_recv.at[side, g],
            device_id=(s, to_t),
            device_id_type=pl.DeviceIdType.MESH,
        )

    has_next = t < tiles - 1
    has_last = t > 0

    def arrive(ref, sem):
        pltpu.make_async_copy(ref, ref, sem).wait()

    @pl.when(s > 0)
    def _():
        @pl.loop(0, 4)
        def _(k):
            g = chunk_at(k)
            arrive(prior.at[g, :, :, 16:32], prior_sem.at[g])

            @pl.when(has_next & (t != tiles // 2 - 1))
            def _():
                halo(t + 1, 0, 0, g).start()

            @pl.when(has_last & (t != tiles // 2))
            def _():
                halo(t - 1, 32, 1, g).start()

    home.wait()
    arrive(bands.at[:, 0:240], cur_sem.at[0])
    arrive(bands.at[:, 0:240], send_sem.at[1])

    @pl.when(s < secs - 1)
    def _():
        arrive(bands, send_sem.at[0])
        arrive(bands.at[:, 0:32], send_sem.at[2])

    @pl.when(s > 0)
    def _():
        @pl.loop(0, 4)
        def _(g):
            @pl.when(has_next & (t != tiles // 2 - 1))
            def _():
                halo(t + 1, 0, 0, g).wait_send()

            @pl.when(has_last & (t != tiles // 2))
            def _():
                halo(t - 1, 32, 1, g).wait_send()

            @pl.when(has_next)
            def _():
                arrive(prior.at[g, :, :, 32:48], halo_recv.at[1, g])

            @pl.when(has_last)
            def _():
                arrive(prior.at[g, :, :, 0:16], halo_recv.at[0, g])


def share(sections, weights):
    hbm = pl.BlockSpec(memory_space=pltpu.HBM)
    return pl.pallas_call(
        share_kernel,
        out_shape=(
            jax.ShapeDtypeStruct((4, 4, 4, 16, 128), BF),
            jax.ShapeDtypeStruct((4, 4, 4, 48, 128), BF),
        ),
        in_specs=[hbm] * 6,
        out_specs=(hbm, hbm),
        scratch_shapes=[
            pltpu.VMEM((ROWS // CHUNK, 8 * CHUNK, 128), BF),
            *[pltpu.VMEM(w.shape, BF) for w in weights],
            pltpu.VMEM((4, ROWS, 128), BF),
            pltpu.VMEM((4, CHUNK, 256), BF),
            pltpu.VMEM((8, 2 * CHUNK, 512), BF),
            pltpu.VMEM((8, CHUNK, 512), BF),
            pltpu.VMEM((4, CHUNK, 256), BF),
            pltpu.VMEM((256, 2048), BF),
            pltpu.VMEM((512, 256), BF),
            pltpu.VMEM((512, 128), BF),
            pltpu.VMEM((256, 256), BF),
            pltpu.VMEM((256, 128), BF),
            pltpu.VMEM((256, 256), BF),
            pltpu.SemaphoreType.DMA((5,)),
            pltpu.SemaphoreType.DMA((ROWS // CHUNK,)),
            pltpu.SemaphoreType.DMA((3,)),
            pltpu.SemaphoreType.DMA((1,)),
            pltpu.SemaphoreType.DMA((4,)),
            pltpu.SemaphoreType.DMA((2, 4)),
            pltpu.SemaphoreType.DMA((2, 4)),
            pltpu.SemaphoreType.DMA,
        ],
        compiler_params=pltpu.CompilerParams(
            vmem_limit_bytes=LIMIT, collective_id=0, has_side_effects=True
        ),
        name="share",
    )(sections, *weights)


def weave(main, *others):
    extra = [step for other in others for step in other]
    used = 0
    for n, step in enumerate(main):
        step()
        goal = len(extra) * (n + 1) // len(main)
        while used < goal:
            extra[used]()
            used += 1


def correlate_kernel(
    shift, cur_hbm, prior_hbm, out_hbm, cur, prior, cur32, wide, lhs, rhs, picked, rows, out, in_sem, out_sem
):
    s = lax.axis_index("sec")
    t = lax.axis_index("tile")
    loads = []
    for i in range(4):
        near = pl.ds(16 * i, 16)
        loads.append(
            (
                pltpu.make_async_copy(prior_hbm.at[near], prior.at[near], in_sem.at[0, i]),
                pltpu.make_async_copy(cur_hbm.at[near], cur.at[near], in_sem.at[1, i]),
            )
        )
    for pair in loads:
        for load in pair:
            load.start()
    wide[0:4] = jnp.zeros((4, 48, 128), F32)
    wide[68:72] = jnp.zeros((4, 48, 128), F32)

    row = iota((1, 48, 128), 1)
    first = jnp.where(t == 0, 16, 0)
    last = jnp.where(t == lax.axis_size("tile") - 1, 32, 48)
    last = jnp.where(s == 0, 0, last)
    inside = (row >= first) & (row < last)

    lane = iota((8, 128), 1)
    slot = lane // 32
    sub = iota((8, 128), 0)
    lane256 = iota((8, 256), 1)
    block = (lane256 % 32) // 8
    wide_lane = iota((32, 128), 1)

    def widen(member):
        def step(i):
            if i == 0:
                for load in loads[member]:
                    load.wait()
            q = 16 * member + 4 * i
            wide[4 + q : 8 + q] = jnp.where(inside, prior[q : q + 4].astype(F32), 0.0)
            cur32[q : q + 4] = cur[q : q + 4].astype(F32)

        return [functools.partial(step, i) for i in range(4)]

    def windows(tile):
        dy = shift[0, tile]

        def step(q):
            here = wide[16 * tile + q, pl.ds(8 + dy, 32), :]
            beside = wide[16 * tile + q + 1, pl.ds(8 + dy, 32), :]
            lhs[tile][0, q] = here.astype(BF)
            for e in range(1, 4):
                mixed = jnp.where(wide_lane < 32 * e, beside, here)
                lhs[tile][e, q] = pltpu.roll(mixed, 128 - 32 * e, 1).astype(BF)

        return [functools.partial(step, q) for q in range(23)]

    def masked(side, j):
        def step(u):
            y = (u % 4 - j) % 4 + 4 * (u // 4)
            for pair in range(2):
                left, right = [], []
                for m in (2 * pair, 2 * pair + 1):
                    q = 32 * side + 8 * j + 2 * m
                    a = jnp.broadcast_to(cur32[q, y : y + 1, :], (8, 128))
                    b = jnp.broadcast_to(cur32[q + 1, y : y + 1, :], (8, 128))
                    left.append(jnp.where(slot == sub, a, 0.0))
                    right.append(jnp.where(slot + 4 == sub, b, 0.0))
                at = u * 32 + 16 * pair
                rhs[j % 2][at : at + 16, 0:128] = jnp.concatenate(left, axis=0).astype(BF)
                rhs[j % 2][at : at + 16, 128:256] = jnp.concatenate(right, axis=0).astype(BF)

        return [functools.partial(step, u) for u in range(16)]

    def products(side, j):
        tile = 2 * side + j // 2
        dx = shift[1, tile]

        def step(group):
            places, parts = [], []
            for jj in group:
                place = 8 + dx + 32 * (j % 2) + jj
                e = lax.rem(place, 4)
                q = lax.div(place, 4)
                for m in range(6 if jj == 0 else 5):
                    places.append(jj + 8 * m)
                    parts.append(
                        jnp.concatenate([lhs[tile][e, q + 2 * m], lhs[tile][e, q + 2 * m + 1]], axis=1)
                    )
            product = lax.dot_general(
                jnp.concatenate(parts, axis=0),
                rhs[j % 2][...],
                (((1,), (1,)), ((), ())),
                preferred_element_type=F32,
            ).reshape(len(parts), 4, 8, 512)
            for jj in group:
                for ox in range(jj, SPAN, 8):
                    at = [places.index(ox + 8 * b) for b in range(4)]
                    for half in range(2):
                        lanes = slice(256 * half, 256 * half + 256)
                        for i in range(3):
                            piece = product[at[3], i + half, :, lanes]
                            for b in (2, 1, 0):
                                piece = jnp.where(block == b, product[at[b], i + half, :, lanes], piece)
                            picked[2 * side + half][j, ox, i] = piece

        return [functools.partial(step, range(g, g + GROUP)) for g in range(0, 8, GROUP)]

    def merge(side, half):
        source = picked[2 * side + half]

        def step(ox):
            for v in range(2):
                for i in range(3):
                    blocks = [source[j, ox, i, :, 128 * v : 128 * v + 128] for j in range(4)]
                    for k in range(4):
                        merged = blocks[(3 - k) % 4]
                        for u in (2, 1, 0):
                            merged = jnp.where(slot == u, blocks[(u - k) % 4], merged)
                        if k:
                            merged = pltpu.roll(merged, 128 - 32 * k, 1)
                        y = 4 * v + k
                        start = ((BASE + 8 * i - y) * SPAN + ox) * 8 + y
                        rows[half][pl.ds(start, 8, stride=8 * SPAN), :] = merged

        return [functools.partial(step, ox) for ox in range(SPAN)]

    sends = []

    def finish(side, half):
        def step(oy):
            start = (BASE + oy) * SPAN * 8
            done = rows[half][start : start + SPAN * 8, :] * (1.0 / math.sqrt(32))
            done = done.astype(BF).reshape(SPAN, 8, 128)
            out[side, oy * SPAN : oy * SPAN + SPAN, 8 * half : 8 * half + 8, :] = done
            if half == 1 and (oy + 1) in SENT:
                part = SENT.index(oy + 1)
                begin = SENT[part - 1] * SPAN if part else 0
                span = pl.ds(begin, (oy + 1) * SPAN - begin)
                send = pltpu.make_async_copy(
                    out.at[side, span],
                    out_hbm.at[span, :, pl.ds(128 * side, 128)],
                    out_sem.at[side, part],
                )
                send.start()
                sends.append(send)

        return [functools.partial(step, oy) for oy in range(SPAN)]

    def run(steps):
        for step in steps:
            step()

    def stage(side, extra, following):
        for j in range(4):
            after = masked(side, j + 1) if j < 3 else following
            weave(products(side, j), after, extra[j])

    def quarters(steps):
        return [steps[len(steps) * n // 4 : len(steps) * (n + 1) // 4] for n in range(4)]

    run(widen(0))
    run(widen(1))
    run(masked(0, 0))
    run(windows(0))
    stage(
        0, [widen(2) + windows(1)[:11], windows(1)[11:] + widen(3), windows(2), windows(3)], masked(1, 0),
    )
    stage(1, quarters(merge(0, 0) + finish(0, 0) + merge(0, 1) + finish(0, 1)), [])
    for half in range(2):
        run(merge(1, half))
        run(finish(1, half))
    for send in sends:
        send.wait()


def correlate(current, prior, tile_shift):
    hbm = pl.BlockSpec(memory_space=pltpu.HBM)
    return pl.pallas_call(
        correlate_kernel,
        out_shape=jax.ShapeDtypeStruct((OFFSETS, 16, 256), BF),
        in_specs=[pl.BlockSpec(memory_space=pltpu.SMEM), hbm, hbm],
        out_specs=hbm,
        scratch_shapes=[
            pltpu.VMEM((64, 16, 128), BF),
            pltpu.VMEM((64, 48, 128), BF),
            pltpu.VMEM((64, 16, 128), F32),
            pltpu.VMEM((72, 48, 128), F32),
            [pltpu.VMEM((4, 24, 32, 128), BF)] * 4,
            [pltpu.VMEM((512, 256), BF)] * 2,
            [pltpu.VMEM((4, SPAN, 3, 8, 256), F32)] * 4,
            [pltpu.VMEM(((BASE + 24) * SPAN * 8, 128), F32)] * 2,
            pltpu.VMEM((2, OFFSETS, 16, 128), BF),
            pltpu.SemaphoreType.DMA((2, 4)),
            pltpu.SemaphoreType.DMA((2, len(SENT))),
        ],
        compiler_params=pltpu.CompilerParams(vmem_limit_bytes=LIMIT),
        name="correlate",
    )(tile_shift, current, prior)


def local(sections, tile_shift, w_first, w_second, w_third, w_fourth, w_fifth):
    weights = (w_first.reshape(2, 2, 32), w_second, w_third, w_fourth, w_fifth.T)
    current, prior = share(sections, weights)
    current = current.reshape(64, 16, 128)
    prior = prior.reshape(64, 48, 128)
    shift = jnp.transpose(tile_shift, (0, 1, 3, 2)).reshape(2, 4)
    found = correlate(current, prior, shift)
    return jnp.transpose(found[None], (0, 2, 1, 3))


def solution(mesh):
    placed = (P("sec", None, "tile"), P("sec", "tile", None, None), P(), P(), P(), P(), P())
    return jax.shard_map(
        local, mesh=mesh, in_specs=placed, out_specs=P("sec", "tile", None, None), check_vma=False
    )
```

time: 32 us -> 28.8 us (0.900)
  the two profiles are of different devices: /device:TPU:57 before, /device:TPU:33 now
where the time goes in v4:
time: 28.8 us; the launch traced here: 28.6 us
  Pallas kernels  28.6 us (99%)
    pallas_call x1, Pallas kernels, share(): pl.pallas_call(share_kernel, out_shape=(jax.ShapeDtypeStruct((4, 4, 4, 16...  20.7 us
    pallas_call x1, Pallas kernels, correlate(): pl.pallas_call(correlate_kernel, out_shape=jax.ShapeDtypeStruct((OFFSETS,...  7.91 us

profile of v4, /device:TPU:33, one launch (start us, length us, event | category | flops | bytes accessed | tf_op | source)
XLA Modules:
  0.0 28.6 jit_solution(8986365720134643408)
XLA Ops:
  0.0 20.7 %share.1 = (bf16[4,4,4,16,128]{4,3,2,1,0:T(8,128)(2,1)}, bf16[4,4,4,48,128]{4,3,2,1,0:T(8,128)(2,1)}) custom-call(bf16[1,2048,128]{2,1,0:T(8,128)(2,1)} %px_hbm.1, bf16[2,2,32]{2,1,0:T(2,128)(2,1)} %bitcast.14, bf16[2,2,32,64]{3,2,1,0:T(8,128)(2,1)} %w2_hbm.1, bf16[2,2,64,64]{3,2,1,0:T(8,128)(2,1)} %w3_hbm.1, bf16[64,64]{1,0:T(8,128)(2,1)} %w4_hbm.1, ...), custom_call_target="tpu_custom_call" | custom-call | tf_op jit(solution)/shard_map/share/pallas_call | solution.py:308
  20.7 7.9 %correlate.1 = bf16[289,16,256]{2,1,0:T(8,128)(2,1)} custom-call(s32[2,4]{1,0:T(2,128)} %bitcast.13, bf16[64,16,128]{2,1,0:T(8,128)(2,1)} %bitcast.11, bf16[64,48,128]{2,1,0:T(8,128)(2,1)} %bitcast.10), custom_call_target="tpu_custom_call" | custom-call | tf_op jit(solution)/shard_map/correlate/pallas_call | solution.py:535

commit v5 on v4

--- a/solution.py
+++ b/solution.py
@@ -20,6 +20,7 @@
 SENT = (6, 12, 17)
 GROUP = 8
 HELD = 1
+LINE = 8 * SPAN + 1
 BASE = 7
 
 
@@ -102,7 +103,8 @@
     a3[:, :, 0:128] = out[:, 0]
     a3[:, :, 128:256] = out[:, 1]
     out = relu(dot(a3[...].reshape(4 * CHUNK, 256), e4[...]))
-    return dot(out, e5[...]).astype(BF).reshape(4, CHUNK, 128)
+    out = dot(out, e5[...]).astype(BF).reshape(4, CHUNK // 16, 16, 128)
+    return jnp.stack([out[:, k] for k in range(CHUNK // 16)])
 
 
 def share_kernel(
@@ -170,7 +172,7 @@
     expand_weights(w1, w2, w3, w4, w5, e1, e2, e3, e4, e5)
 
     def band_of(to_t):
-        return bands.at[:, pl.ds(pl.multiple_of(16 * to_t, 16), 16)]
+        return bands.at[to_t]
 
     home = pltpu.make_async_copy(band_of(t), cur.at[member, group], home_sem)
 
@@ -178,7 +180,7 @@
         chunk = chunk_at(phase)
         fetch(phase).wait()
         done = encode_chunk(px.at[phase], xs, a1, a2, a3, e1, e2, e3, e4, e5, perm)
-        bands[:, pl.ds(pl.multiple_of(chunk * CHUNK, CHUNK), CHUNK), :] = done
+        bands[pl.ds(chunk * (CHUNK // 16), CHUNK // 16)] = done
 
     def send_phase(phase):
         chunk = chunk_at(phase)
@@ -198,15 +200,15 @@
             @pl.loop(0, CHUNK // 16)
             def _(k):
                 to_t = chunk * (CHUNK // 16) + lax.rem(k + member, CHUNK // 16)
-                push(to_t, (s + 1, to_t), 0, prior.at[member, group, :, 16:32], prior_sem.at[member])
+                push(to_t, (s + 1, to_t), 0, prior.at[1, member, group], prior_sem.at[member])
 
                 @pl.when(to_t == tiles // 2 - 1)
                 def _():
-                    push(to_t, (s + 1, to_t + 1), 2, prior.at[member, group, :, 0:16], halo_recv.at[0, member])
+                    push(to_t, (s + 1, to_t + 1), 2, prior.at[0, member, group], halo_recv.at[0, member])
 
                 @pl.when(to_t == tiles // 2)
                 def _():
-                    push(to_t, (s + 1, to_t - 1), 2, prior.at[member, group, :, 32:48], halo_recv.at[1, member])
+                    push(to_t, (s + 1, to_t - 1), 2, prior.at[2, member, group], halo_recv.at[1, member])
 
         @pl.loop(0, CHUNK // 16)
         def _(k):
@@ -242,10 +244,10 @@
         def _():
             send_phase(phase)
 
-    def halo(to_t, row, side, g):
+    def halo(to_t, part, side, g):
         return pltpu.make_async_remote_copy(
-            src_ref=prior.at[g, :, :, 16:32],
-            dst_ref=prior.at[g, :, :, row : row + 16],
+            src_ref=prior.at[1, g],
+            dst_ref=prior.at[part, g],
             send_sem=halo_send.at[side, g],
             recv_sem=halo_recv.at[side, g],
             device_id=(s, to_t),
@@ -263,7 +265,7 @@
         @pl.loop(0, 4)
         def _(k):
             g = chunk_at(k)
-            arrive(prior.at[g, :, :, 16:32], prior_sem.at[g])
+            arrive(prior.at[1, g], prior_sem.at[g])
 
             @pl.when(has_next & (t != tiles // 2 - 1))
             def _():
@@ -271,16 +273,16 @@
 
             @pl.when(has_last & (t != tiles // 2))
             def _():
-                halo(t - 1, 32, 1, g).start()
+                halo(t - 1, 2, 1, g).start()
 
     home.wait()
-    arrive(bands.at[:, 0:240], cur_sem.at[0])
-    arrive(bands.at[:, 0:240], send_sem.at[1])
+    arrive(bands.at[0:15], cur_sem.at[0])
+    arrive(bands.at[0:15], send_sem.at[1])
 
     @pl.when(s < secs - 1)
     def _():
         arrive(bands, send_sem.at[0])
-        arrive(bands.at[:, 0:32], send_sem.at[2])
+        arrive(bands.at[0:2], send_sem.at[2])
 
     @pl.when(s > 0)
     def _():
@@ -292,15 +294,15 @@
 
             @pl.when(has_last & (t != tiles // 2))
             def _():
-                halo(t - 1, 32, 1, g).wait_send()
+                halo(t - 1, 2, 1, g).wait_send()
 
             @pl.when(has_next)
             def _():
-                arrive(prior.at[g, :, :, 32:48], halo_recv.at[1, g])
+                arrive(prior.at[2, g], halo_recv.at[1, g])
 
             @pl.when(has_last)
             def _():
-                arrive(prior.at[g, :, :, 0:16], halo_recv.at[0, g])
+                arrive(prior.at[0, g], halo_recv.at[0, g])
 
 
 def share(sections, weights):
@@ -309,14 +311,14 @@
         share_kernel,
         out_shape=(
             jax.ShapeDtypeStruct((4, 4, 4, 16, 128), BF),
-            jax.ShapeDtypeStruct((4, 4, 4, 48, 128), BF),
+            jax.ShapeDtypeStruct((3, 4, 4, 4, 16, 128), BF),
         ),
         in_specs=[hbm] * 6,
         out_specs=(hbm, hbm),
         scratch_shapes=[
             pltpu.VMEM((ROWS // CHUNK, 8 * CHUNK, 128), BF),
             *[pltpu.VMEM(w.shape, BF) for w in weights],
-            pltpu.VMEM((4, ROWS, 128), BF),
+            pltpu.VMEM((ROWS // 16, 4, 16, 128), BF),
             pltpu.VMEM((4, CHUNK, 256), BF),
             pltpu.VMEM((8, 2 * CHUNK, 512), BF),
             pltpu.VMEM((8, CHUNK, 512), BF),
@@ -355,7 +357,7 @@
 
 
 def correlate_kernel(
-    shift, cur_hbm, prior_hbm, out_hbm, cur, prior, cur32, wide, lhs, rhs, picked, rows, out, in_sem, out_sem
+    shift, cur_hbm, prior_hbm, out_hbm, cur, prior, cur32, wide, both, above, below, rhs, picked, rows, out, in_sem, out_sem
 ):
     s = lax.axis_index("sec")
     t = lax.axis_index("tile")
@@ -364,7 +366,7 @@
         near = pl.ds(16 * i, 16)
         loads.append(
             (
-                pltpu.make_async_copy(prior_hbm.at[near], prior.at[near], in_sem.at[0, i]),
+                pltpu.make_async_copy(prior_hbm.at[:, near], prior.at[:, near], in_sem.at[0, i]),
                 pltpu.make_async_copy(cur_hbm.at[near], cur.at[near], in_sem.at[1, i]),
             )
         )
@@ -374,11 +376,7 @@
     wide[0:4] = jnp.zeros((4, 48, 128), F32)
     wide[68:72] = jnp.zeros((4, 48, 128), F32)
 
-    row = iota((1, 48, 128), 1)
-    first = jnp.where(t == 0, 16, 0)
-    last = jnp.where(t == lax.axis_size("tile") - 1, 32, 48)
-    last = jnp.where(s == 0, 0, last)
-    inside = (row >= first) & (row < last)
+    inside = [(s > 0) & (t > 0), s > 0, (s > 0) & (t < lax.axis_size("tile") - 1)]
 
     lane = iota((8, 128), 1)
     slot = lane // 32
@@ -393,21 +391,33 @@
                 for load in loads[member]:
                     load.wait()
             q = 16 * member + 4 * i
-            wide[4 + q : 8 + q] = jnp.where(inside, prior[q : q + 4].astype(F32), 0.0)
+            for part in range(3):
+                values = prior[part, q : q + 4].astype(F32)
+                wide[4 + q : 8 + q, 16 * part : 16 * part + 16] = jnp.where(inside[part], values, 0.0)
             cur32[q : q + 4] = cur[q : q + 4].astype(F32)
 
         return [functools.partial(step, i) for i in range(4)]
 
     def windows(tile):
         dy = shift[0, tile]
+        kept = {}
 
         def step(q):
             here = wide[16 * tile + q, pl.ds(8 + dy, 32), :]
             beside = wide[16 * tile + q + 1, pl.ds(8 + dy, 32), :]
-            lhs[tile][0, q] = here.astype(BF)
+            kept[q] = [here]
             for e in range(1, 4):
                 mixed = jnp.where(wide_lane < 32 * e, beside, here)
-                lhs[tile][e, q] = pltpu.roll(mixed, 128 - 32 * e, 1).astype(BF)
+                kept[q].append(pltpu.roll(mixed, 128 - 32 * e, 1))
+            for e in range(4):
+                both[tile][e, q] = kept[q][e][8:24].astype(BF)
+            for first in [q - 2] + ([q - 1, q] if q == 22 else []):
+                if first >= 0:
+                    second = min(first + 2, 22)
+                    for e in range(4):
+                        for rows_of, at in ((above, 0), (below, 24)):
+                            pair = [kept[first][e][at : at + 8], kept[second][e][at : at + 8]]
+                            rows_of[tile][e, first] = jnp.concatenate(pair, axis=0).astype(BF)
 
         return [functools.partial(step, q) for q in range(23)]
 
@@ -432,32 +442,50 @@
         tile = 2 * side + j // 2
         dx = shift[1, tile]
 
+        def times(parts, weights):
+            return lax.dot_general(
+                jnp.concatenate(parts, axis=0),
+                weights,
+                (((1,), (1,)), ((), ())),
+                preferred_element_type=F32,
+            ).reshape(len(parts), 2, 8, weights.shape[0])
+
         def step(group):
-            places, parts = [], []
+            places, parts, pairs, tops, ends = [], [], [], [], []
             for jj in group:
                 place = 8 + dx + 32 * (j % 2) + jj
                 e = lax.rem(place, 4)
                 q = lax.div(place, 4)
+
+                def window(source, m):
+                    return jnp.concatenate([source[tile][e, q + 2 * m], source[tile][e, q + 2 * m + 1]], axis=1)
+
                 for m in range(6 if jj == 0 else 5):
                     places.append(jj + 8 * m)
-                    parts.append(
-                        jnp.concatenate([lhs[tile][e, q + 2 * m], lhs[tile][e, q + 2 * m + 1]], axis=1)
-                    )
-            product = lax.dot_general(
-                jnp.concatenate(parts, axis=0),
-                rhs[j % 2][...],
-                (((1,), (1,)), ((), ())),
-                preferred_element_type=F32,
-            ).reshape(len(parts), 4, 8, 512)
+                    parts.append(window(both, m))
+                for m in range(0, 6, 2):
+                    pairs += [jj + 8 * m, jj + 8 * m + 8]
+                    tops.append(window(above, m))
+                    ends.append(window(below, m))
+            weights = rhs[j % 2]
+            middle = times(parts, weights[...])
+            top = times(tops, weights[0:256])
+            end = times(ends, weights[256:512])
+
+            def rows_at(place, half, i):
+                if i + half == 0:
+                    return top[pairs.index(place) // 2, pairs.index(place) % 2]
+                if i + half == 3:
+                    return end[pairs.index(place) // 2, pairs.index(place) % 2]
+                return middle[places.index(place), i + half - 1, :, 256 * half : 256 * half + 256]
+
             for jj in group:
                 for ox in range(jj, SPAN, 8):
-                    at = [places.index(ox + 8 * b) for b in range(4)]
                     for half in range(2):
-                        lanes = slice(256 * half, 256 * half + 256)
                         for i in range(3):
-                            piece = product[at[3], i + half, :, lanes]
+                            piece = rows_at(ox + 24, half, i)
                             for b in (2, 1, 0):
-                                piece = jnp.where(block == b, product[at[b], i + half, :, lanes], piece)
+                                piece = jnp.where(block == b, rows_at(ox + 8 * b, half, i), piece)
                             picked[2 * side + half][j, ox, i] = piece
 
         return [functools.partial(step, range(g, g + GROUP)) for g in range(0, 8, GROUP)]
@@ -476,8 +504,8 @@
                         if k:
                             merged = pltpu.roll(merged, 128 - 32 * k, 1)
                         y = 4 * v + k
-                        start = ((BASE + 8 * i - y) * SPAN + ox) * 8 + y
-                        rows[half][pl.ds(start, 8, stride=8 * SPAN), :] = merged
+                        start = (BASE + 8 * i - y) * LINE + ox * 8 + y
+                        rows[half][pl.ds(start, 8, stride=LINE), :] = merged
 
         return [functools.partial(step, ox) for ox in range(SPAN)]
 
@@ -485,7 +513,7 @@
 
     def finish(side, half):
         def step(oy):
-            start = (BASE + oy) * SPAN * 8
+            start = (BASE + oy) * LINE
             done = rows[half][start : start + SPAN * 8, :] * (1.0 / math.sqrt(32))
             done = done.astype(BF).reshape(SPAN, 8, 128)
             out[side, oy * SPAN : oy * SPAN + SPAN, 8 * half : 8 * half + 8, :] = done
@@ -519,8 +547,9 @@
     run(widen(1))
     run(masked(0, 0))
     run(windows(0))
+    beside = windows(1)
     stage(
-        0, [widen(2) + windows(1)[:11], windows(1)[11:] + widen(3), windows(2), windows(3)], masked(1, 0),
+        0, [widen(2) + beside[:11], beside[11:] + widen(3), windows(2), windows(3)], masked(1, 0),
     )
     stage(1, quarters(merge(0, 0) + finish(0, 0) + merge(0, 1) + finish(0, 1)), [])
     for half in range(2):
@@ -539,13 +568,15 @@
         out_specs=hbm,
         scratch_shapes=[
             pltpu.VMEM((64, 16, 128), BF),
-            pltpu.VMEM((64, 48, 128), BF),
+            pltpu.VMEM((3, 64, 16, 128), BF),
             pltpu.VMEM((64, 16, 128), F32),
             pltpu.VMEM((72, 48, 128), F32),
-            [pltpu.VMEM((4, 24, 32, 128), BF)] * 4,
+            [pltpu.VMEM((4, 24, 16, 128), BF)] * 4,
+            [pltpu.VMEM((4, 24, 16, 128), BF)] * 4,
+            [pltpu.VMEM((4, 24, 16, 128), BF)] * 4,
             [pltpu.VMEM((512, 256), BF)] * 2,
             [pltpu.VMEM((4, SPAN, 3, 8, 256), F32)] * 4,
-            [pltpu.VMEM(((BASE + 24) * SPAN * 8, 128), F32)] * 2,
+            [pltpu.VMEM(((BASE + 24) * LINE, 128), F32)] * 2,
             pltpu.VMEM((2, OFFSETS, 16, 128), BF),
             pltpu.SemaphoreType.DMA((2, 4)),
             pltpu.SemaphoreType.DMA((2, len(SENT))),
@@ -559,7 +590,7 @@
     weights = (w_first.reshape(2, 2, 32), w_second, w_third, w_fourth, w_fifth.T)
     current, prior = share(sections, weights)
     current = current.reshape(64, 16, 128)
-    prior = prior.reshape(64, 48, 128)
+    prior = prior.reshape(3, 64, 16, 128)
     shift = jnp.transpose(tile_shift, (0, 1, 3, 2)).reshape(2, 4)
     found = correlate(current, prior, shift)
     return jnp.transpose(found[None], (0, 2, 1, 3))

time: 28.8 us -> 28.2 us (0.979)
  Pallas kernels: 28.6 us -> 28 us
    pallas_call x1, Pallas kernels: 7.91 us -> 7.33 us  [correlate(): pl.pallas_call(correlate_kernel, out_shape=jax.ShapeDtypeStruct((OFFSETS,...]
where the time goes in v5:
time: 28.2 us; the launch traced here: 28 us
  Pallas kernels  28 us (99%)
    pallas_call x1, Pallas kernels, share(): pl.pallas_call(share_kernel, out_shape=(jax.ShapeDtypeStruct((4, 4, 4, 16...  20.7 us
    pallas_call x1, Pallas kernels, correlate(): pl.pallas_call(correlate_kernel, out_shape=jax.ShapeDtypeStruct((OFFSETS,...  7.33 us

profile of v5, /device:TPU:33, one launch (start us, length us, event | category | flops | bytes accessed | tf_op | source)
XLA Modules:
  0.0 28.0 jit_solution(11741927257329845174)
XLA Ops:
  0.0 20.7 %share.1 = (bf16[4,4,4,16,128]{4,3,2,1,0:T(8,128)(2,1)}, bf16[3,4,4,4,16,128]{5,4,3,2,1,0:T(8,128)(2,1)}) custom-call(bf16[1,2048,128]{2,1,0:T(8,128)(2,1)} %px_hbm.1, bf16[2,2,32]{2,1,0:T(2,128)(2,1)} %bitcast.14, bf16[2,2,32,64]{3,2,1,0:T(8,128)(2,1)} %w2_hbm.1, bf16[2,2,64,64]{3,2,1,0:T(8,128)(2,1)} %w3_hbm.1, bf16[64,64]{1,0:T(8,128)(2,1)} %w4_hbm.1, ...), custom_call_target="tpu_custom_call" | custom-call | tf_op jit(solution)/shard_map/share/pallas_call | solution.py:310
  20.7 7.3 %correlate.1 = bf16[289,16,256]{2,1,0:T(8,128)(2,1)} custom-call(s32[2,4]{1,0:T(2,128)} %bitcast.13, bf16[64,16,128]{2,1,0:T(8,128)(2,1)} %bitcast.11, bf16[3,64,16,128]{3,2,1,0:T(8,128)(2,1)} %bitcast.10), custom_call_target="tpu_custom_call" | custom-call | tf_op jit(solution)/shard_map/correlate/pallas_call | solution.py:564

commit v6 on v5

--- a/solution.py
+++ b/solution.py
@@ -576,7 +576,7 @@
             [pltpu.VMEM((4, 24, 16, 128), BF)] * 4,
             [pltpu.VMEM((512, 256), BF)] * 2,
             [pltpu.VMEM((4, SPAN, 3, 8, 256), F32)] * 4,
-            [pltpu.VMEM(((BASE + 24) * LINE, 128), F32)] * 2,
+            [pltpu.VMEM(((BASE + 25) * LINE, 128), F32)] * 2,
             pltpu.VMEM((2, OFFSETS, 16, 128), BF),
             pltpu.SemaphoreType.DMA((2, 4)),
             pltpu.SemaphoreType.DMA((2, len(SENT))),

time: 28.2 us -> 28.2 us (level)
  no operation moved by 1% of the time
where the time goes in v6:
time: 28.2 us; the launch traced here: 28 us
  Pallas kernels  28 us (99%)
    pallas_call x1, Pallas kernels, share(): pl.pallas_call(share_kernel, out_shape=(jax.ShapeDtypeStruct((4, 4, 4, 16...  20.7 us
    pallas_call x1, Pallas kernels, correlate(): pl.pallas_call(correlate_kernel, out_shape=jax.ShapeDtypeStruct((OFFSETS,...  7.31 us

profile of v6, /device:TPU:33, one launch (start us, length us, event | category | flops | bytes accessed | tf_op | source)
XLA Modules:
  0.0 28.0 jit_solution(14987417155077728302)
XLA Ops:
  0.0 20.7 %share.1 = (bf16[4,4,4,16,128]{4,3,2,1,0:T(8,128)(2,1)}, bf16[3,4,4,4,16,128]{5,4,3,2,1,0:T(8,128)(2,1)}) custom-call(bf16[1,2048,128]{2,1,0:T(8,128)(2,1)} %px_hbm.1, bf16[2,2,32]{2,1,0:T(2,128)(2,1)} %bitcast.14, bf16[2,2,32,64]{3,2,1,0:T(8,128)(2,1)} %w2_hbm.1, bf16[2,2,64,64]{3,2,1,0:T(8,128)(2,1)} %w3_hbm.1, bf16[64,64]{1,0:T(8,128)(2,1)} %w4_hbm.1, ...), custom_call_target="tpu_custom_call" | custom-call | tf_op jit(solution)/shard_map/share/pallas_call | solution.py:310
  20.7 7.3 %correlate.1 = bf16[289,16,256]{2,1,0:T(8,128)(2,1)} custom-call(s32[2,4]{1,0:T(2,128)} %bitcast.13, bf16[64,16,128]{2,1,0:T(8,128)(2,1)} %bitcast.11, bf16[3,64,16,128]{3,2,1,0:T(8,128)(2,1)} %bitcast.10), custom_call_target="tpu_custom_call" | custom-call | tf_op jit(solution)/shard_map/correlate/pallas_call | solution.py:564

commit v7 on v6

--- a/solution.py
+++ b/solution.py
@@ -134,13 +134,13 @@
             barrier, inc=1, device_id=(to_s, to_t), device_id_type=pl.DeviceIdType.MESH
         )
 
-    @pl.loop(1, tiles)
+    @pl.loop(1, tiles, unroll=True)
     def _(k):
         greet(s, lax.rem(t + k, tiles))
 
     @pl.when(s > 0)
     def _():
-        @pl.loop(0, tiles)
+        @pl.loop(0, tiles, unroll=True)
         def _(k):
             greet(s - 1, lax.rem(t + k, tiles))
 

time: 28.2 us -> 28.1 us (level)
  no operation moved by 1% of the time
where the time goes in v7:
time: 28.1 us; the launch traced here: 27.9 us
  Pallas kernels  27.9 us (99%)
    pallas_call x1, Pallas kernels, share(): pl.pallas_call(share_kernel, out_shape=(jax.ShapeDtypeStruct((4, 4, 4, 16...  20.6 us
    pallas_call x1, Pallas kernels, correlate(): pl.pallas_call(correlate_kernel, out_shape=jax.ShapeDtypeStruct((OFFSETS,...  7.31 us

profile of v7, /device:TPU:33, one launch (start us, length us, event | category | flops | bytes accessed | tf_op | source)
XLA Modules:
  0.0 27.9 jit_solution(282077390954496791)
XLA Ops:
  0.0 20.6 %share.1 = (bf16[4,4,4,16,128]{4,3,2,1,0:T(8,128)(2,1)}, bf16[3,4,4,4,16,128]{5,4,3,2,1,0:T(8,128)(2,1)}) custom-call(bf16[1,2048,128]{2,1,0:T(8,128)(2,1)} %px_hbm.1, bf16[2,2,32]{2,1,0:T(2,128)(2,1)} %bitcast.14, bf16[2,2,32,64]{3,2,1,0:T(8,128)(2,1)} %w2_hbm.1, bf16[2,2,64,64]{3,2,1,0:T(8,128)(2,1)} %w3_hbm.1, bf16[64,64]{1,0:T(8,128)(2,1)} %w4_hbm.1, ...), custom_call_target="tpu_custom_call" | custom-call | tf_op jit(solution)/shard_map/share/pallas_call | solution.py:310
  20.6 7.3 %correlate.1 = bf16[289,16,256]{2,1,0:T(8,128)(2,1)} custom-call(s32[2,4]{1,0:T(2,128)} %bitcast.13, bf16[64,16,128]{2,1,0:T(8,128)(2,1)} %bitcast.11, bf16[3,64,16,128]{3,2,1,0:T(8,128)(2,1)} %bitcast.10), custom_call_target="tpu_custom_call" | custom-call | tf_op jit(solution)/shard_map/correlate/pallas_call | solution.py:564
